TPU v7x, 512 devices: a whole 4x4x16 slice. The times are simulated.
512 devices in a mesh: tm: 64 (over x_hi, z, core), height: 8 (over y, x_lo).
Axes of the slice: x: 4 (x_hi: 2, x_lo: 2; x = x_hi * 2 + x_lo), y: 4, z: 16, core: 2. Of those that a mesh axis runs over, the one named last changes fastest.
Arguments:
- queries: bfloat16 [384, 32, 6, 1536], P('tm', 'height'), may hold values from -6 to 6
- keys: bfloat16 [384, 32, 6, 1536], P('tm', 'height'), may hold values from -6 to 6
- values: bfloat16 [384, 32, 6, 1536], P('tm', 'height'), may hold values from -6 to 6
- grad_out: bfloat16 [384, 32, 6, 1536], P('tm', 'height'), may hold values from -6 to 6
- reach: int32 [2, 12], replicated, may hold values from 0 to 1, as said below
Outputs:
- attn_out: bfloat16 [384, 32, 6, 1536], P('tm', 'height')
- grad_queries: bfloat16 [384, 32, 6, 1536], P('tm', 'height')
- grad_keys: bfloat16 [384, 32, 6, 1536], P('tm', 'height')
- grad_values: bfloat16 [384, 32, 6, 1536], P('tm', 'height')
Inputs may be any that keep to these rules, and one draw needn't show every extreme that they name: `reach`: in each row exactly half of the 12 heads have 1.
All inputs are finite; a program needn't handle non-finite values.
Results may differ from a plain program's by a relative error of at most 0.024.
Values may be sent and summed in bfloat16 or wider, within the bound.
A program may use at most 128 MiB of HBM per device.

v0:
```python
import jax
import jax.numpy as jnp
from jax import lax
from jax.sharding import PartitionSpec as P


def from_partner(block, axis, stride):
    count = lax.axis_size(axis)
    route = []
    for low in range(count):
        high = low | 1 << stride
        if high != low and high < count:
            route += [(low, high), (high, low)]
    return lax.ppermute(block, axis, route)


def from_behind(block, axis, distance):
    devices = range(lax.axis_size(axis))
    route = [(i - distance, i) for i in devices if i - distance in devices]
    return lax.ppermute(block, axis, route)


def window_mask(reach, spans, tile_steps, clip_pos, clip_count, block):
    allowed = (spans[None, :] >= -reach[0][:, None]) & (spans[None, :] <= reach[1][:, None])
    inside = (clip_pos + tile_steps >= 0) & (clip_pos + tile_steps < clip_count)
    allowed = allowed & inside[None, :]
    head_count = reach.shape[1]
    return jnp.broadcast_to(allowed[:, :, None], (head_count, spans.shape[0], block)).reshape(
        head_count, spans.shape[0] * block
    )


def to_heads(flat, head_count):
    return flat.reshape(flat.shape[0], head_count, -1).transpose(1, 0, 2)


def from_heads(headed):
    return headed.transpose(1, 0, 2).reshape(headed.shape[1], -1)


def local(queries, keys, values, grad_out, reach):
    head_count = reach.shape[1]
    channels = queries.shape[-1]
    head_size = channels // head_count
    factor = head_size ** (-0.5)
    tokens = queries.shape[0] * queries.shape[1] * queries.shape[2]
    flat_q = queries.reshape(tokens, channels)
    flat_k = keys.reshape(tokens, channels)
    flat_v = values.reshape(tokens, channels)
    flat_d = grad_out.reshape(tokens, channels)
    clip_count = lax.axis_size("tm")
    clip_pos = lax.axis_index("tm")
    partner_k, partner_v = from_partner((flat_k, flat_v), "height", 0)
    tile_k = jnp.concatenate([flat_k, partner_k], axis=0)
    tile_v = jnp.concatenate([flat_v, partner_v], axis=0)
    shifted = [from_behind((tile_k, tile_v), "tm", offset) for offset in (1, -1)]
    win_k = jnp.concatenate([shifted[0][0], tile_k, shifted[1][0]], axis=0)
    win_v = jnp.concatenate([shifted[0][1], tile_v, shifted[1][1]], axis=0)
    three_steps = jnp.arange(3, dtype=jnp.int32) - 1
    key_mask = window_mask(reach, three_steps, three_steps, clip_pos, clip_count, 2 * tokens)[
        :, None, :
    ]
    query_heads = to_heads(flat_q, head_count)
    grad_heads = to_heads(flat_d, head_count)
    key_heads = to_heads(win_k, head_count)
    value_heads = to_heads(win_v, head_count)
    scores = (
        jnp.einsum("hqd,hkd->hqk", query_heads, key_heads, preferred_element_type=jnp.float32)
        * factor
    )
    masked = jnp.where(key_mask, scores, -1e30)
    row_max = jnp.max(masked, axis=-1)
    log_total = row_max + jnp.log(jnp.sum(jnp.exp(masked - row_max[..., None]), axis=-1))
    probability = jnp.where(key_mask, jnp.exp(scores - log_total[..., None]), 0.0)
    weights = probability.astype(jnp.bfloat16)
    attended = jnp.einsum(
        "hqk,hkd->hqd", weights, value_heads, preferred_element_type=jnp.float32
    ).astype(jnp.bfloat16)
    row_dot = jnp.einsum("hqd,hqd->hq", grad_heads, attended, preferred_element_type=jnp.float32)
    grad_prob = jnp.einsum(
        "hqd,hkd->hqk", grad_heads, value_heads, preferred_element_type=jnp.float32
    )
    grad_score = (probability * (grad_prob - row_dot[..., None])).astype(jnp.bfloat16)
    grad_query = (
        jnp.einsum("hqk,hkd->hqd", grad_score, key_heads, preferred_element_type=jnp.float32)
        * factor
    ).astype(jnp.bfloat16)
    key_parts = (
        jnp.einsum("hqk,hqd->hkd", grad_score, query_heads, preferred_element_type=jnp.float32)
        * factor
    ).astype(jnp.bfloat16)
    value_parts = jnp.einsum(
        "hqk,hqd->hkd", weights, grad_heads, preferred_element_type=jnp.float32
    ).astype(jnp.bfloat16)
    key_parts = from_heads(key_parts).reshape(3, 2 * tokens, channels)
    value_parts = from_heads(value_parts).reshape(3, 2 * tokens, channels)
    returned = [
        from_behind((key_parts[block_id], value_parts[block_id]), "tm", offset)
        for offset, block_id in ((1, 2), (-1, 0))
    ]
    key_total = (
        key_parts[1].astype(jnp.float32)
        + returned[0][0].astype(jnp.float32)
        + returned[1][0].astype(jnp.float32)
    )
    value_total = (
        value_parts[1].astype(jnp.float32)
        + returned[0][1].astype(jnp.float32)
        + returned[1][1].astype(jnp.float32)
    )
    partner_key, partner_value = (
        from_partner(key_total[tokens:].astype(jnp.bfloat16), "height", 0).astype(jnp.float32),
        from_partner(value_total[tokens:].astype(jnp.bfloat16), "height", 0).astype(jnp.float32),
    )
    grad_key = (key_total[:tokens] + partner_key).astype(jnp.bfloat16)
    grad_value = (value_total[:tokens] + partner_value).astype(jnp.bfloat16)
    out_shape = queries.shape
    return (
        from_heads(attended).reshape(out_shape),
        from_heads(grad_query).reshape(out_shape),
        grad_key.reshape(out_shape),
        grad_value.reshape(out_shape),
    )


def solution(mesh):
    return jax.shard_map(
        local,
        mesh=mesh,
        in_specs=(
            P("tm", "height", None, None),
            P("tm", "height", None, None),
            P("tm", "height", None, None),
            P("tm", "height", None, None),
            P(),
        ),
        out_specs=(
            P("tm", "height", None, None),
            P("tm", "height", None, None),
            P("tm", "height", None, None),
            P("tm", "height", None, None),
        ),
        check_vma=False,
    )
```

profile of v0, /device:TPU:463, one launch (start us, length us, event | category | flops | bytes accessed | tf_op | source)
XLA Modules:
  0.0 130.5 jit_solution(1062842505899785658)
XLA Ops:
  0.7 1.2 copy.40
  1.8 0.9 reshape.147
  2.7 2.4 %collective-permute-start = (bf16[144,1536]{1,0:T(8,128)(2,1)}, bf16[144,1536]{1,0:T(8,128)(2,1)S(1)}, u32[]{:S(2)}, u32[]{:S(2)}) collective-permute-start(bf16[144,1536]{1,0:T(8,128)(2,1)} %reshape.147), channel_id=1, source_target_pairs={{0,1},{1,0},{2,3},{3,2},{4,5},{5,4},{6,7},{7,6},{8,9},{9,8},{10,11... | collective-permute-start | bytes 1327112 | tf_op jit(solution)/shard_map/ppermute | solution.py:14
  5.2 1.1 copy.48
  6.3 0.9 reshape.148
  7.2 2.8 %collective-permute-start.3 = (bf16[144,1536]{1,0:T(8,128)(2,1)}, bf16[144,1536]{1,0:T(8,128)(2,1)S(1)}, u32[]{:S(2)}, u32[]{:S(2)}) collective-permute-start(bf16[144,1536]{1,0:T(8,128)(2,1)} %reshape.148), channel_id=1, source_target_pairs={{0,1},{1,0},{2,3},{3,2},{4,5},{5,4},{6,7},{7,6},{8,9},{9,8},{10,11... | collective-permute-start | bytes 1327112 | tf_op jit(solution)/shard_map/ppermute | solution.py:14
  11.5 0.9 copy.43
  12.4 0.9 copy.51
  13.9 1.3 %copy.55 = bf16[6,4,6,1536]{3,2,1,0:T(8,128)(2,1)S(1)} copy(bf16[6,4,6,1536]{3,1,2,0:T(4,128)(2,1)} %param.8) | data formatting | bytes 884736 | tf_op args[3]
  15.8 1.0 constant_dynamic-update-slice_fusion.1
  16.9 3.6 %collective-permute-start.2 = (bf16[288,1536]{1,0:T(8,128)(2,1)S(1)}, bf16[288,1536]{1,0:T(8,128)(2,1)S(1)}, u32[]{:S(2)}, u32[]{:S(2)}) collective-permute-start(bf16[288,1536]{1,0:T(8,128)(2,1)S(1)} %constant_dynamic-update-slice_fusion), channel_id=1, source_target_pairs={{8,0},{16,8},{24,16},{32,24},{40,32},{48,40},{56,48},{64,56},{72,6... | collective-permute-start | bytes 2654216 | tf_op jit(solution)/shard_map/ppermute | solution.py:20
  20.5 1.0 constant_dynamic-update-slice_fusion.3
  21.6 2.5 %collective-permute-start.1 = (bf16[288,1536]{1,0:T(8,128)(2,1)S(1)}, bf16[288,1536]{1,0:T(8,128)(2,1)S(1)}, u32[]{:S(2)}, u32[]{:S(2)}) collective-permute-start(bf16[288,1536]{1,0:T(8,128)(2,1)S(1)} %constant_dynamic-update-slice_fusion), channel_id=1, source_target_pairs={{0,8},{8,16},{16,24},{24,32},{32,40},{40,48},{48,56},{56,64},{64,7... | collective-permute-start | bytes 2654216 | tf_op jit(solution)/shard_map/ppermute | solution.py:20
  24.1 1.2 collective-permute-done.3
  25.4 3.5 %collective-permute-start.5 = (bf16[288,1536]{1,0:T(8,128)(2,1)S(1)}, bf16[288,1536]{1,0:T(8,128)(2,1)S(1)}, u32[]{:S(2)}, u32[]{:S(2)}) collective-permute-start(bf16[288,1536]{1,0:T(8,128)(2,1)S(1)} %constant_dynamic-update-slice_fusion.2), channel_id=1, source_target_pairs={{8,0},{16,8},{24,16},{32,24},{40,32},{48,40},{56,48},{64,56},{72,6... | collective-permute-start | bytes 2654216 | tf_op jit(solution)/shard_map/ppermute | solution.py:20
  28.8 21.5 %collective-permute-start.4 = (bf16[288,1536]{1,0:T(8,128)(2,1)S(1)}, bf16[288,1536]{1,0:T(8,128)(2,1)S(1)}, u32[]{:S(2)}, u32[]{:S(2)}) collective-permute-start(bf16[288,1536]{1,0:T(8,128)(2,1)S(1)} %constant_dynamic-update-slice_fusion.2), channel_id=1, source_target_pairs={{0,8},{8,16},{16,24},{24,32},{32,40},{40,48},{48,56},{56,64},{64,7... | collective-permute-start | bytes 2654216 | tf_op jit(solution)/shard_map/ppermute | solution.py:20
  50.9 2.8 %bitcast_reduce_fusion = (f32[12,144]{1,0:T(8,128)S(1)}, f32[12,864,144]{1,2,0:T(8,128)S(1)}) fusion(pred[12,864]{1,0:T(8,128)(4,1)S(1)} %broadcast_in_dim.33, bf16[12,144,128]{2,0,1:T(8,128)(2,1)S(1)} %bitcast.101, bf16[288,12,128]{2,0,1:T(8,128)(2,1)S(1)} %copy_bitcast_fusion.6, bf16[144,12,128]{2,0,1:T(8,128)(2,1)S(1)} %copy_bitcast_fusion.9, ...), kind=kOutput, calls=%fused_computation.1 | convolution fusion | flops 397300032 | bytes 9085824 | tf_op jit(solution)/shard_map/hqd,hkd->hqk/dot_general | solution.py:68
  53.8 1.9 %fusion.1 = f32[12,144]{1,0:T(8,128)S(1)} fusion(f32[12,864,144]{1,2,0:T(8,128)S(1)} %get-tuple-element.21, f32[12,144]{1,0:T(8,128)S(1)} %get-tuple-element.20, pred[12,864]{1,0:T(8,128)(4,1)S(1)} %broadcast_in_dim.33), kind=kLoop, calls=%fused_computation.3 | loop fusion | flops 5970240 | bytes 5996160 | tf_op jit(solution)/shard_map/reduce_sum | solution.py:73
  55.7 3.5 %collective-permute-done.5 = bf16[288,1536]{1,0:T(8,128)(2,1)S(1)} collective-permute-done((bf16[288,1536]{1,0:T(8,128)(2,1)S(1)}, bf16[288,1536]{1,0:T(8,128)(2,1)S(1)}, u32[]{:S(2)}, u32[]{:S(2)}) %collective-permute-start.5) | collective-permute-done | bytes 884768 | tf_op jit(solution)/shard_map/ppermute | solution.py:20
  59.3 1.0 collective-permute-done.4
  60.5 2.7 %fusion.25 = (f32[12,144,128]{2,1,0:T(8,128)S(1)}, bf16[12,144,128]{2,1,0:T(8,128)(2,1)}) fusion(bf16[288,12,128]{2,0,1:T(8,128)(2,1)S(1)} %copy_bitcast_fusion.4, bf16[144,12,128]{2,0,1:T(8,128)(2,1)S(1)} %copy_bitcast_fusion.8, bf16[144,12,128]{2,0,1:T(8,128)(2,1)S(1)} %copy-done.15, bf16[288,12,128]{2,0,1:T(8,128)(2,1)S(1)} %copy_bitcast_fusion.5, ...), kind=kOutput, calls=%fused_computation.66 | convolution fusion | flops 399237120 | bytes 9970560 | tf_op jit(solution)/shard_map/hqk,hkd->hqd/dot_general | solution.py:76
  64.4 5.4 %convert_bitcast_fusion = bf16[864,12,128]{2,0,1:T(8,128)(2,1)S(1)} fusion(bf16[12,144,128]{2,0,1:T(8,128)(2,1)S(1)} %bitcast.99, f32[12,864,144]{1,2,0:T(8,128)} %copy-done, f32[12,144]{1,0:T(8,128)} %copy-done.20, pred[12,864]{1,0:T(8,128)(4,1)} %copy-done.18), kind=kOutput, calls=%fused_computation.11 | convolution fusion | flops 389505024 | bytes 9085824 | tf_op jit(solution)/shard_map/hqk,hqd->hkd/dot_general | solution.py:92
  69.9 2.4 %multiply_convert_fusion = bf16[12,864,144]{1,2,0:T(8,128)(2,1)S(1)} fusion(f32[12,864,144]{1,2,0:T(8,128)S(1)} %bitcast.98, f32[12,144]{1,0:T(8,128)S(1)} %copy-done.22, f32[12,144]{1,0:T(8,128)S(1)} %copy-done.21, pred[12,864]{1,0:T(8,128)(4,1)S(1)} %copy-done.19, bf16[288,12,128]{2,0,1:T(8,128)(2,1)S(1)} %copy_bitcast_fusion.4, ...), kind=kOutput, calls=%fused_computation.4 | convolution fusion | flops 401780736 | bytes 12078720 | tf_op jit(solution)/shard_map/hqd,hkd->hqk/dot_general | solution.py:80
  72.5 1.1 copy.111
  73.6 1.1 copy.110
  74.7 2.1 %collective-permute-start.10 = (bf16[288,1536]{1,0:T(8,128)(2,1)}, bf16[288,1536]{1,0:T(8,128)(2,1)}, u32[]{:S(2)}, u32[]{:S(2)}) collective-permute-start(bf16[288,1536]{1,0:T(8,128)(2,1)} %bitcast.93), channel_id=1, source_target_pairs={{8,0},{16,8},{24,16},{32,24},{40,32},{48,40},{56,48},{64,56},{72,6... | collective-permute-start | bytes 2654216 | tf_op jit(solution)/shard_map/ppermute | solution.py:20
  76.8 4.4 %collective-permute-start.9 = (bf16[288,1536]{1,0:T(8,128)(2,1)}, bf16[288,1536]{1,0:T(8,128)(2,1)}, u32[]{:S(2)}, u32[]{:S(2)}) collective-permute-start(bf16[288,1536]{1,0:T(8,128)(2,1)} %bitcast.94), channel_id=1, source_target_pairs={{0,8},{8,16},{16,24},{24,32},{32,40},{40,48},{48,56},{56,64},{64,7... | collective-permute-start | bytes 2654216 | tf_op jit(solution)/shard_map/ppermute | solution.py:20
  81.2 1.8 %fusion.3 = bf16[864,12,128]{2,0,1:T(8,128)(2,1)S(1)} fusion(bf16[12,864,144]{1,2,0:T(8,128)(2,1)S(1)} %multiply_convert_fusion, bf16[12,144,128]{2,0,1:T(8,128)(2,1)S(1)} %bitcast.102), kind=kOutput, calls=%fused_computation.8 | convolution fusion | flops 384860160 | bytes 6082560 | tf_op jit(solution)/shard_map/hqk,hqd->hkd/dot_general | solution.py:89
  83.3 1.1 copy.113
  84.4 1.1 copy.112
  85.6 1.9 %collective-permute-start.7 = (bf16[288,1536]{1,0:T(8,128)(2,1)}, bf16[288,1536]{1,0:T(8,128)(2,1)}, u32[]{:S(2)}, u32[]{:S(2)}) collective-permute-start(bf16[288,1536]{1,0:T(8,128)(2,1)} %bitcast.95), channel_id=1, source_target_pairs={{8,0},{16,8},{24,16},{32,24},{40,32},{48,40},{56,48},{64,56},{72,6... | collective-permute-start | bytes 2654216 | tf_op jit(solution)/shard_map/ppermute | solution.py:20
  87.5 3.8 %collective-permute-start.6 = (bf16[288,1536]{1,0:T(8,128)(2,1)}, bf16[288,1536]{1,0:T(8,128)(2,1)}, u32[]{:S(2)}, u32[]{:S(2)}) collective-permute-start(bf16[288,1536]{1,0:T(8,128)(2,1)} %bitcast.96), channel_id=1, source_target_pairs={{0,8},{8,16},{16,24},{24,32},{32,40},{40,48},{48,56},{56,64},{64,7... | collective-permute-start | bytes 2654216 | tf_op jit(solution)/shard_map/ppermute | solution.py:20
  91.3 2.0 %fusion.7 = bf16[144,12,128]{2,0,1:T(8,128)(2,1)} fusion(bf16[12,864,144]{1,2,0:T(8,128)(2,1)S(1)} %multiply_convert_fusion, bf16[288,12,128]{2,0,1:T(8,128)(2,1)S(1)} %copy-done.2, bf16[144,12,128]{2,0,1:T(8,128)(2,1)S(1)} %copy-done.10, bf16[144,12,128]{2,0,1:T(8,128)(2,1)S(1)} %copy-done.14, bf16[288,12,128]{2,0,1:T(8,128)(2,1)S(1)} %copy-done.4), kind=kOutput, calls=%fused_computation.21 | convolution fusion | flops 393265152 | bytes 6082560 | tf_op jit(solution)/shard_map/hqk,hkd->hqd/dot_general | solution.py:85
  93.3 1.0 copy.54
  94.3 2.3 %reshape_reshape.15 = bf16[6,4,6,1536]{3,2,1,0:T(8,128)(2,1)} reshape(bf16[144,12,128]{2,1,0:T(8,128)(2,1)} %copy.54) | data formatting | bytes 884736 | tf_op jit(solution)/shard_map/reshape;reshape | solution.py:119
  96.6 2.1 %copy.66 = bf16[6,4,6,1536]{3,1,2,0:T(4,128)(2,1)} copy(bf16[6,4,6,1536]{3,2,1,0:T(8,128)(2,1)} %reshape_reshape.15) | data formatting | bytes 884736
  98.6 2.0 %copy.57 = bf16[144,12,128]{2,1,0:T(8,128)(2,1)} copy(bf16[144,12,128]{2,0,1:T(8,128)(2,1)} %fusion.7) | data formatting | bytes 884736 | tf_op jit(solution)/shard_map/convert_element_type | solution.py:87
  100.6 2.3 %reshape_reshape.17 = bf16[6,4,6,1536]{3,2,1,0:T(8,128)(2,1)} reshape(bf16[144,12,128]{2,1,0:T(8,128)(2,1)} %copy.57) | data formatting | bytes 884736 | tf_op jit(solution)/shard_map/reshape;reshape | solution.py:120
  102.9 2.1 %copy.67 = bf16[6,4,6,1536]{3,1,2,0:T(4,128)(2,1)} copy(bf16[6,4,6,1536]{3,2,1,0:T(8,128)(2,1)} %reshape_reshape.17) | data formatting | bytes 884736
  105.0 1.7 %fusion.4 = f32[288,1536]{1,0:T(8,128)S(1)} fusion(f32[12,36,8,128]{3,2,1,0:T(8,128)S(1)} %get-tuple-element.14, bf16[288,1536]{1,0:T(8,128)(2,1)} %collective-permute-done.10, bf16[288,1536]{1,0:T(8,128)(2,1)} %collective-permute-done.9), kind=kLoop, calls=%fused_computation.13 | loop fusion | flops 1769472 | bytes 5308416 | tf_op jit(solution)/shard_map/add | solution.py:107
  106.7 2.5 %collective-permute-start.11 = (bf16[144,1536]{1,0:T(8,128)(2,1)S(1)}, bf16[144,1536]{1,0:T(8,128)(2,1)S(1)}, u32[]{:S(2)}, u32[]{:S(2)}) collective-permute-start(bf16[144,1536]{1,0:T(8,128)(2,1)S(1)} %slice.82), channel_id=1, source_target_pairs={{0,1},{1,0},{2,3},{3,2},{4,5},{5,4},{6,7},{7,6},{8,9},{9,8},{10,11... | collective-permute-start | bytes 1327112 | tf_op jit(solution)/shard_map/ppermute | solution.py:14
  109.2 1.7 %fusion.5 = f32[288,1536]{1,0:T(8,128)S(1)} fusion(f32[12,36,8,128]{3,2,1,0:T(8,128)S(1)} %get-tuple-element.17, bf16[288,1536]{1,0:T(8,128)(2,1)} %collective-permute-done.7, bf16[288,1536]{1,0:T(8,128)(2,1)} %collective-permute-done.6), kind=kLoop, calls=%fused_computation.15 | loop fusion | flops 1769472 | bytes 5308416 | tf_op jit(solution)/shard_map/add | solution.py:102
  110.9 0.8 slice.83
  111.7 2.8 %collective-permute-start.8 = (bf16[144,1536]{1,0:T(8,128)(2,1)}, bf16[144,1536]{1,0:T(8,128)(2,1)S(1)}, u32[]{:S(2)}, u32[]{:S(2)}) collective-permute-start(bf16[144,1536]{1,0:T(8,128)(2,1)} %slice.83), channel_id=1, source_target_pairs={{0,1},{1,0},{2,3},{3,2},{4,5},{5,4},{6,7},{7,6},{8,9},{9,8},{10,11... | collective-permute-start | bytes 1327112 | tf_op jit(solution)/shard_map/ppermute | solution.py:14
  114.5 6.2 %collective-permute-done.11 = bf16[144,1536]{1,0:T(8,128)(2,1)S(1)} collective-permute-done((bf16[144,1536]{1,0:T(8,128)(2,1)S(1)}, bf16[144,1536]{1,0:T(8,128)(2,1)S(1)}, u32[]{:S(2)}, u32[]{:S(2)}) %collective-permute-start.11) | collective-permute-done | bytes 442400 | tf_op jit(solution)/shard_map/ppermute | solution.py:14
  121.0 1.0 copy.69
  122.0 7.2 %collective-permute-done.8 = bf16[144,1536]{1,0:T(8,128)(2,1)S(1)} collective-permute-done((bf16[144,1536]{1,0:T(8,128)(2,1)}, bf16[144,1536]{1,0:T(8,128)(2,1)S(1)}, u32[]{:S(2)}, u32[]{:S(2)}) %collective-permute-start.8) | collective-permute-done | bytes 442400 | tf_op jit(solution)/shard_map/ppermute | solution.py:14
  129.5 1.0 copy.68
  (90 shorter events, 5.7 us)
Async XLA Ops:
  0.6 10.5 %copy-start.23 = (s32[2,12]{1,0:T(2,128)S(1)}, s32[2,12]{1,0:T(2,128)}, u32[]{:S(2)}) copy-start(s32[2,12]{1,0:T(2,128)} %param.9) | copy-start | bytes 292
  0.6 12.7 %copy-start.13 = (bf16[6,4,6,1536]{3,1,2,0:T(4,128)(2,1)S(1)}, bf16[6,4,6,1536]{3,1,2,0:T(4,128)(2,1)}, u32[]{:S(2)}) copy-start(bf16[6,4,6,1536]{3,1,2,0:T(4,128)(2,1)} %param.5) | copy-start | bytes 1327108
  2.7 14.1 %collective-permute-start = (bf16[144,1536]{1,0:T(8,128)(2,1)}, bf16[144,1536]{1,0:T(8,128)(2,1)S(1)}, u32[]{:S(2)}, u32[]{:S(2)}) collective-permute-start(bf16[144,1536]{1,0:T(8,128)(2,1)} %reshape.147), channel_id=1, source_target_pairs={{0,1},{1,0},{2,3},{3,2},{4,5},{5,4},{6,7},{7,6},{8,9},{9,8},{10,11... | collective-permute-start | bytes 1327112 | tf_op jit(solution)/shard_map/ppermute | solution.py:14
  7.2 18.1 %collective-permute-start.3 = (bf16[144,1536]{1,0:T(8,128)(2,1)}, bf16[144,1536]{1,0:T(8,128)(2,1)S(1)}, u32[]{:S(2)}, u32[]{:S(2)}) collective-permute-start(bf16[144,1536]{1,0:T(8,128)(2,1)} %reshape.148), channel_id=1, source_target_pairs={{0,1},{1,0},{2,3},{3,2},{4,5},{5,4},{6,7},{7,6},{8,9},{9,8},{10,11... | collective-permute-start | bytes 1327112 | tf_op jit(solution)/shard_map/ppermute | solution.py:14
  11.5 48.9 %copy-start.18 = (pred[12,864]{1,0:T(8,128)(4,1)}, pred[12,864]{1,0:T(8,128)(4,1)S(1)}, u32[]{:S(2)}) copy-start(pred[12,864]{1,0:T(8,128)(4,1)S(1)} %broadcast_in_dim.33) | copy-start | bytes 31108
  13.9 37.0 %copy-start.7 = (bf16[144,12,128]{2,1,0:T(8,128)(2,1)}, bf16[144,12,128]{2,1,0:T(8,128)(2,1)S(1)}, u32[]{:S(2)}) copy-start(bf16[144,12,128]{2,1,0:T(8,128)(2,1)S(1)} %reshape_reshape.14) | copy-start | bytes 1327108
  16.9 33.7 %collective-permute-start.2 = (bf16[288,1536]{1,0:T(8,128)(2,1)S(1)}, bf16[288,1536]{1,0:T(8,128)(2,1)S(1)}, u32[]{:S(2)}, u32[]{:S(2)}) collective-permute-start(bf16[288,1536]{1,0:T(8,128)(2,1)S(1)} %constant_dynamic-update-slice_fusion), channel_id=1, source_target_pairs={{8,0},{16,8},{24,16},{32,24},{40,32},{48,40},{56,48},{64,56},{72,6... | collective-permute-start | bytes 2654216 | tf_op jit(solution)/shard_map/ppermute | solution.py:20
  21.6 29.2 %collective-permute-start.1 = (bf16[288,1536]{1,0:T(8,128)(2,1)S(1)}, bf16[288,1536]{1,0:T(8,128)(2,1)S(1)}, u32[]{:S(2)}, u32[]{:S(2)}) collective-permute-start(bf16[288,1536]{1,0:T(8,128)(2,1)S(1)} %constant_dynamic-update-slice_fusion), channel_id=1, source_target_pairs={{0,8},{8,16},{16,24},{24,32},{32,40},{40,48},{48,56},{56,64},{64,7... | collective-permute-start | bytes 2654216 | tf_op jit(solution)/shard_map/ppermute | solution.py:20
  25.4 33.8 %collective-permute-start.5 = (bf16[288,1536]{1,0:T(8,128)(2,1)S(1)}, bf16[288,1536]{1,0:T(8,128)(2,1)S(1)}, u32[]{:S(2)}, u32[]{:S(2)}) collective-permute-start(bf16[288,1536]{1,0:T(8,128)(2,1)S(1)} %constant_dynamic-update-slice_fusion.2), channel_id=1, source_target_pairs={{8,0},{16,8},{24,16},{32,24},{40,32},{48,40},{56,48},{64,56},{72,6... | collective-permute-start | bytes 2654216 | tf_op jit(solution)/shard_map/ppermute | solution.py:20
  28.8 31.5 %collective-permute-start.4 = (bf16[288,1536]{1,0:T(8,128)(2,1)S(1)}, bf16[288,1536]{1,0:T(8,128)(2,1)S(1)}, u32[]{:S(2)}, u32[]{:S(2)}) collective-permute-start(bf16[288,1536]{1,0:T(8,128)(2,1)S(1)} %constant_dynamic-update-slice_fusion.2), channel_id=1, source_target_pairs={{0,8},{8,16},{16,24},{24,32},{32,40},{40,48},{48,56},{56,64},{64,7... | collective-permute-start | bytes 2654216 | tf_op jit(solution)/shard_map/ppermute | solution.py:20
  50.4 3.3 %copy-start.9 = (bf16[144,12,128]{2,0,1:T(8,128)(2,1)}, bf16[144,12,128]{2,0,1:T(8,128)(2,1)S(1)}, u32[]{:S(2)}) copy-start(bf16[144,12,128]{2,0,1:T(8,128)(2,1)S(1)} %copy_bitcast_fusion.9) | copy-start | bytes 1327108
  50.5 10.0 %copy-start.11 = (bf16[144,12,128]{2,0,1:T(8,128)(2,1)}, bf16[144,12,128]{2,0,1:T(8,128)(2,1)S(1)}, u32[]{:S(2)}) copy-start(bf16[144,12,128]{2,0,1:T(8,128)(2,1)S(1)} %copy_bitcast_fusion.8) | copy-start | bytes 1327108
  50.7 3.0 %copy-start.1 = (bf16[288,12,128]{2,0,1:T(8,128)(2,1)}, bf16[288,12,128]{2,0,1:T(8,128)(2,1)S(1)}, u32[]{:S(2)}) copy-start(bf16[288,12,128]{2,0,1:T(8,128)(2,1)S(1)} %copy_bitcast_fusion.6) | copy-start | bytes 2654212
  50.9 2.8 %copy-start.3 = (bf16[288,12,128]{2,0,1:T(8,128)(2,1)}, bf16[288,12,128]{2,0,1:T(8,128)(2,1)S(1)}, u32[]{:S(2)}) copy-start(bf16[288,12,128]{2,0,1:T(8,128)(2,1)S(1)} %copy_bitcast_fusion.7) | copy-start | bytes 2654212
  53.7 9.5 %copy-start = (f32[12,864,144]{1,2,0:T(8,128)}, f32[12,864,144]{1,2,0:T(8,128)S(1)}, u32[]{:S(2)}) copy-start(f32[12,864,144]{1,2,0:T(8,128)S(1)} %get-tuple-element.21) | copy-start | bytes 17915908
  53.7 6.8 %copy-start.15 = (bf16[144,12,128]{2,0,1:T(8,128)(2,1)S(1)}, bf16[144,12,128]{2,0,1:T(8,128)(2,1)}, u32[]{:S(2)}) copy-start(bf16[144,12,128]{2,0,1:T(8,128)(2,1)} %copy.51) | copy-start | bytes 1327108
  55.7 7.6 %copy-start.20 = (f32[12,144]{1,0:T(8,128)}, f32[12,144]{1,0:T(8,128)S(1)}, u32[]{:S(2)}) copy-start(f32[12,144]{1,0:T(8,128)S(1)} %log_add_fusion) | copy-start | bytes 20740
  60.5 2.7 %copy-start.5 = (bf16[288,12,128]{2,0,1:T(8,128)(2,1)}, bf16[288,12,128]{2,0,1:T(8,128)(2,1)S(1)}, u32[]{:S(2)}) copy-start(bf16[288,12,128]{2,0,1:T(8,128)(2,1)S(1)} %copy_bitcast_fusion.5) | copy-start | bytes 2654212
  63.2 6.6 %slice-start = ((s8[6193152]{0:T(1024)(128)(4,1)}), s8[1998848]{0:T(1024)(128)(4,1)S(1)}, s32[]{:S(2)}) async-start(s8[6193152]{0:T(1024)(128)(4,1)} %bitcast.97), calls=%async_computation | async-start | bytes 3997696
  64.3 5.5 %slice-start.1 = ((s8[6193152]{0:T(1024)(128)(4,1)}), s8[4194304]{0:T(1024)(128)(4,1)S(1)}, s32[]{:S(2)}) async-start(s8[6193152]{0:T(1024)(128)(4,1)} %bitcast.97), calls=%async_computation.1 | async-start | bytes 8388608
  64.3 5.5 %copy-start.6 = (bf16[288,12,128]{2,0,1:T(8,128)(2,1)S(1)}, bf16[288,12,128]{2,0,1:T(8,128)(2,1)}, u32[]{:S(2)}) copy-start(bf16[288,12,128]{2,0,1:T(8,128)(2,1)} %copy-done.5) | copy-start | bytes 2654212
  64.3 5.5 %copy-start.12 = (bf16[144,12,128]{2,0,1:T(8,128)(2,1)S(1)}, bf16[144,12,128]{2,0,1:T(8,128)(2,1)}, u32[]{:S(2)}) copy-start(bf16[144,12,128]{2,0,1:T(8,128)(2,1)} %copy-done.11) | copy-start | bytes 1327108
  64.3 5.5 %copy-start.16 = (bf16[144,12,128]{2,0,1:T(8,128)(2,1)S(1)}, bf16[144,12,128]{2,0,1:T(8,128)(2,1)}, u32[]{:S(2)}) copy-start(bf16[144,12,128]{2,0,1:T(8,128)(2,1)} %copy.51) | copy-start | bytes 1327108
  64.3 5.5 %copy-start.19 = (pred[12,864]{1,0:T(8,128)(4,1)S(1)}, pred[12,864]{1,0:T(8,128)(4,1)}, u32[]{:S(2)}) copy-start(pred[12,864]{1,0:T(8,128)(4,1)} %copy-done.18) | copy-start | bytes 31108
  64.3 5.5 %copy-start.21 = (f32[12,144]{1,0:T(8,128)S(1)}, f32[12,144]{1,0:T(8,128)}, u32[]{:S(2)}) copy-start(f32[12,144]{1,0:T(8,128)} %copy-done.20) | copy-start | bytes 20740
  64.4 5.5 %copy-start.22 = (f32[12,144]{1,0:T(8,128)S(1)}, f32[12,144]{1,0:T(8,128)}, u32[]{:S(2)}) copy-start(f32[12,144]{1,0:T(8,128)} %copy.74) | copy-start | bytes 20740
  72.2 9.0 %copy-start.8 = (bf16[144,12,128]{2,1,0:T(8,128)(2,1)S(1)}, bf16[144,12,128]{2,1,0:T(8,128)(2,1)}, u32[]{:S(2)}) copy-start(bf16[144,12,128]{2,1,0:T(8,128)(2,1)} %copy-done.7) | copy-start | bytes 1327108
  74.7 30.3 %collective-permute-start.10 = (bf16[288,1536]{1,0:T(8,128)(2,1)}, bf16[288,1536]{1,0:T(8,128)(2,1)}, u32[]{:S(2)}, u32[]{:S(2)}) collective-permute-start(bf16[288,1536]{1,0:T(8,128)(2,1)} %bitcast.93), channel_id=1, source_target_pairs={{8,0},{16,8},{24,16},{32,24},{40,32},{48,40},{56,48},{64,56},{72,6... | collective-permute-start | bytes 2654216 | tf_op jit(solution)/shard_map/ppermute | solution.py:20
  76.8 28.2 %collective-permute-start.9 = (bf16[288,1536]{1,0:T(8,128)(2,1)}, bf16[288,1536]{1,0:T(8,128)(2,1)}, u32[]{:S(2)}, u32[]{:S(2)}) collective-permute-start(bf16[288,1536]{1,0:T(8,128)(2,1)} %bitcast.94), channel_id=1, source_target_pairs={{0,8},{8,16},{16,24},{24,32},{32,40},{40,48},{48,56},{56,64},{64,7... | collective-permute-start | bytes 2654216 | tf_op jit(solution)/shard_map/ppermute | solution.py:20
  83.0 8.3 %copy-start.2 = (bf16[288,12,128]{2,0,1:T(8,128)(2,1)S(1)}, bf16[288,12,128]{2,0,1:T(8,128)(2,1)}, u32[]{:S(2)}) copy-start(bf16[288,12,128]{2,0,1:T(8,128)(2,1)} %copy-done.1) | copy-start | bytes 2654212
  83.0 8.3 %copy-start.4 = (bf16[288,12,128]{2,0,1:T(8,128)(2,1)S(1)}, bf16[288,12,128]{2,0,1:T(8,128)(2,1)}, u32[]{:S(2)}) copy-start(bf16[288,12,128]{2,0,1:T(8,128)(2,1)} %copy-done.3) | copy-start | bytes 2654212
  83.0 8.3 %copy-start.10 = (bf16[144,12,128]{2,0,1:T(8,128)(2,1)S(1)}, bf16[144,12,128]{2,0,1:T(8,128)(2,1)}, u32[]{:S(2)}) copy-start(bf16[144,12,128]{2,0,1:T(8,128)(2,1)} %copy-done.9) | copy-start | bytes 1327108
  83.1 8.3 %copy-start.14 = (bf16[144,12,128]{2,0,1:T(8,128)(2,1)S(1)}, bf16[144,12,128]{2,0,1:T(8,128)(2,1)}, u32[]{:S(2)}) copy-start(bf16[144,12,128]{2,0,1:T(8,128)(2,1)} %copy.43) | copy-start | bytes 1327108
  85.6 23.6 %collective-permute-start.7 = (bf16[288,1536]{1,0:T(8,128)(2,1)}, bf16[288,1536]{1,0:T(8,128)(2,1)}, u32[]{:S(2)}, u32[]{:S(2)}) collective-permute-start(bf16[288,1536]{1,0:T(8,128)(2,1)} %bitcast.95), channel_id=1, source_target_pairs={{8,0},{16,8},{24,16},{32,24},{40,32},{48,40},{56,48},{64,56},{72,6... | collective-permute-start | bytes 2654216 | tf_op jit(solution)/shard_map/ppermute | solution.py:20
  87.5 5.8 %copy-start.17 = (bf16[12,144,128]{2,1,0:T(8,128)(2,1)S(1)}, bf16[12,144,128]{2,1,0:T(8,128)(2,1)}, u32[]{:S(2)}) copy-start(bf16[12,144,128]{2,1,0:T(8,128)(2,1)} %get-tuple-element.23) | copy-start | bytes 1327108
  87.5 21.7 %collective-permute-start.6 = (bf16[288,1536]{1,0:T(8,128)(2,1)}, bf16[288,1536]{1,0:T(8,128)(2,1)}, u32[]{:S(2)}, u32[]{:S(2)}) collective-permute-start(bf16[288,1536]{1,0:T(8,128)(2,1)} %bitcast.96), channel_id=1, source_target_pairs={{0,8},{8,16},{16,24},{24,32},{32,40},{40,48},{48,56},{56,64},{64,7... | collective-permute-start | bytes 2654216 | tf_op jit(solution)/shard_map/ppermute | solution.py:20
  106.7 14.0 %collective-permute-start.11 = (bf16[144,1536]{1,0:T(8,128)(2,1)S(1)}, bf16[144,1536]{1,0:T(8,128)(2,1)S(1)}, u32[]{:S(2)}, u32[]{:S(2)}) collective-permute-start(bf16[144,1536]{1,0:T(8,128)(2,1)S(1)} %slice.82), channel_id=1, source_target_pairs={{0,1},{1,0},{2,3},{3,2},{4,5},{5,4},{6,7},{7,6},{8,9},{9,8},{10,11... | collective-permute-start | bytes 1327112 | tf_op jit(solution)/shard_map/ppermute | solution.py:14
  111.7 17.5 %collective-permute-start.8 = (bf16[144,1536]{1,0:T(8,128)(2,1)}, bf16[144,1536]{1,0:T(8,128)(2,1)S(1)}, u32[]{:S(2)}, u32[]{:S(2)}) collective-permute-start(bf16[144,1536]{1,0:T(8,128)(2,1)} %slice.83), channel_id=1, source_target_pairs={{0,1},{1,0},{2,3},{3,2},{4,5},{5,4},{6,7},{7,6},{8,9},{9,8},{10,11... | collective-permute-start | bytes 1327112 | tf_op jit(solution)/shard_map/ppermute | solution.py:14
where the time goes:
time: 131 us; the launch traced here: 130 us
  starting transfers between devices  53.8 us (41%)
  local copies, waits for them, and re-layouts  32.6 us (25%)
  waiting for transfers between devices  19.2 us (15%)
  matrix products  17 us (13%)
  other arithmetic  6.48 us (5%)
  between operations  1.39 us (1%)
    ppermute x8, starting transfers between devices, from_behind(): return lax.ppermute(block, axis, route)  43.3 us
    ppermute x4, waiting for transfers between devices, from_partner(): return lax.ppermute(block, axis, route)  14.7 us
    unnamed x62, local copies, waits for them, and re-layouts  12 us
    ppermute x4, starting transfers between devices, from_partner(): return lax.ppermute(block, axis, route)  10.5 us
    dot_general x1, matrix products, local(): jnp.einsum('hqk,hqd->hkd', weights, grad_heads, preferred_element_type=jn...  5.42 us
    ppermute x8, waiting for transfers between devices, from_behind(): return lax.ppermute(block, axis, route)  4.52 us
    dot_general x1, matrix products, local(): jnp.einsum('hqd,hkd->hqk', query_heads, key_heads, preferred_element_type...  2.77 us
    dot_general x1, matrix products, local(): jnp.einsum('hqk,hkd->hqd', weights, value_heads, preferred_element_type=j...  2.68 us
  transfers between devices with their start and end apart: 12, of which 5 were waited for; matrix products, arithmetic and copies ran while one was open for 29% of the time, Pallas kernels for 0%

commit v1 on v0

v1 whole, which is shorter than its diff:
```python
import functools
import math

import jax
import jax.numpy as jnp
from jax import lax
from jax.experimental import pallas as pl
from jax.experimental.pallas import tpu as pltpu
from jax.sharding import PartitionSpec as P

MESH = pl.DeviceIdType.MESH
HEADS, SIZE = 12, 128
FRAMES, ROWS, COLS = 6, 4, 6
OWN = HEADS // 2
HALF = (FRAMES, COLS, ROWS, SIZE)
TOKENS = 2 * FRAMES * COLS * ROWS
FACTOR = SIZE**-0.5
FACTOR2 = FACTOR * math.log2(math.e)
RING = 32


def dot(a, b, over_a, over_b):
    return lax.dot_general(
        a, b, (((over_a,), (over_b,)), ((), ())), preferred_element_type=jnp.float32
    )


def one_head(q, d, ks, vs, biases):
    scores = [dot(q, k, 1, 1) for k in ks]
    scores = [s if b is None else s + b for s, b in zip(scores, biases)]
    top = functools.reduce(jnp.maximum, [jnp.max(s, axis=1, keepdims=True) for s in scores])
    raised = [jnp.exp2((s - top) * FACTOR2) for s in scores]
    total = sum(jnp.sum(e, axis=1, keepdims=True) for e in raised)
    inverse = 1.0 / total
    probability = [e * inverse for e in raised]
    weights = [p.astype(jnp.bfloat16) for p in probability]
    attended = sum(dot(w, v, 1, 0) for w, v in zip(weights, vs)).astype(jnp.bfloat16)
    row_dot = jnp.sum(
        attended.astype(jnp.float32) * d.astype(jnp.float32), axis=1, keepdims=True
    )
    grad_prob = [dot(d, v, 1, 1) for v in vs]
    grad_score = [
        (p * (g - row_dot)).astype(jnp.bfloat16) for p, g in zip(probability, grad_prob)
    ]
    grad_query = sum(dot(s, k, 1, 0) for s, k in zip(grad_score, ks)) * FACTOR
    key_parts = [dot(s, q, 0, 0) * FACTOR for s in grad_score]
    value_parts = [dot(w, d, 0, 0) for w in weights]
    return attended, grad_query.astype(jnp.bfloat16), key_parts, value_parts


def kernel(
    reach, k_in, v_in, q_in, d_in, o_out, dq_out, dk_out, dv_out,
    tile, near, local_grad, sent, got, done,
    own_sem, xs_sem, xr_sem, ks_sem, kr_sem, gs_sem, gr_sem, os_sem, or_sem, ol_sem,
):
    tm, height = lax.axis_index("tm"), lax.axis_index("height")
    count = lax.axis_size("tm")
    inputs = (k_in, v_in, q_in, d_in)
    outputs = (o_out, dq_out, dk_out, dv_out)
    other = height + 1 - 2 * (height % 2)
    partner = (tm, other)
    flip_next = (tm % RING + 1) // RING
    flip_prev = 1 - (tm % RING + RING - 1) // RING
    following = ((tm + 1) % count, height + flip_next * (other - height))
    preceding = ((tm + count - 1) % count, height + flip_prev * (other - height))
    side = (height % 2 + tm // RING) % 2
    mine, theirs = side * OWN, (1 - side) * OWN

    def own_copy(j, a):
        return pltpu.make_async_copy(
            inputs[a].at[:, :, mine + j], tile.at[j, a, 0], own_sem.at[j, a]
        )

    def remote(src, dst, send, recv, device):
        return pltpu.make_async_remote_copy(
            src_ref=src, dst_ref=dst, send_sem=send, recv_sem=recv, device_id=device,
            device_id_type=MESH,
        )

    def half_copy(j, a):
        return remote(
            inputs[a].at[:, :, theirs + j], tile.at[j, a, 1], xs_sem.at[j, a], xr_sem.at[j, a], partner
        )

    def key_copies(j):
        block = tile.at[j, pl.ds(0, 2)]
        return (
            remote(block, near.at[j, 0], ks_sem.at[j, 0], kr_sem.at[j, 0], following),
            remote(block, near.at[j, 1], ks_sem.at[j, 1], kr_sem.at[j, 1], preceding),
        )

    def grad_copies(j):
        return (
            remote(sent.at[j, 1], got.at[j, 0], gs_sem.at[j, 0], gr_sem.at[j, 0], following),
            remote(sent.at[j, 0], got.at[j, 1], gs_sem.at[j, 1], gr_sem.at[j, 1], preceding),
        )

    def out_own(j, a):
        return pltpu.make_async_copy(
            done.at[j, a, 0], outputs[a].at[:, :, mine + j], ol_sem.at[j, a]
        )

    def out_half(j, a):
        return remote(
            done.at[j, a, 1], outputs[a].at[:, :, mine + j], os_sem.at[j, a], or_sem.at[j, a], partner
        )

    def out_half_in(j, a):
        return remote(
            done.at[j, a, 1], outputs[a].at[:, :, theirs + j], os_sem.at[j, a], or_sem.at[j, a], partner
        )

    barrier = pltpu.get_barrier_semaphore()
    for device in (partner, following, preceding):
        pl.semaphore_signal(barrier, inc=1, device_id=device, device_id_type=MESH)
    pl.semaphore_wait(barrier, 3)

    def begin(j, carry):
        for a in range(4):
            half_copy(j, a).start()
        for a in range(4):
            own_copy(j, a).start()
        return carry

    lax.fori_loop(0, OWN, begin, 0)

    def flat(x):
        return x.reshape(TOKENS, SIZE)

    def tiled(x):
        return x.astype(jnp.bfloat16).reshape((2,) + HALF)

    def step(it, carry):
        @pl.when(it < OWN)
        def _():
            j = it
            for a in range(4):
                own_copy(j, a).wait()
                half_copy(j, a).wait_recv()
            for copy in key_copies(j):
                copy.start()

        @pl.when((it >= 1) & (it < OWN + 1))
        def _():
            j = it - 1
            for copy in key_copies(j):
                copy.wait_recv()
            k, v, q, d = [flat(tile[j, a]) for a in range(4)]
            ks = [k, flat(near[j, 0, 0]), flat(near[j, 1, 0])]
            vs = [v, flat(near[j, 0, 1]), flat(near[j, 1, 1])]
            back = (reach[0, mine + j] >= 1) & (tm >= 1)
            ahead = (reach[1, mine + j] >= 1) & (tm < count - 1)
            biases = [None, jnp.where(back, 0.0, -1e30), jnp.where(ahead, 0.0, -1e30)]
            attended, grad_query, key_parts, value_parts = one_head(q, d, ks, vs, biases)
            done[j, 0] = tiled(attended)
            done[j, 1] = tiled(grad_query)
            local_grad[j % 2, 0] = key_parts[0]
            local_grad[j % 2, 1] = value_parts[0]
            for way in range(2):
                sent[j, way, 0] = tiled(key_parts[1 + way])
                sent[j, way, 1] = tiled(value_parts[1 + way])
            for copy in grad_copies(j):
                copy.start()
            for a in range(2):
                out_half(j, a).start()
                out_own(j, a).start()

        @pl.when(it >= 2)
        def _():
            j = it - 2
            for copy in grad_copies(j):
                copy.wait_recv()
            for part in range(2):
                total = local_grad[j % 2, part]
                for way in range(2):
                    total = total + flat(got[j, way, part]).astype(jnp.float32)
                done[j, 2 + part] = tiled(total)
            for a in range(2, 4):
                out_half(j, a).start()
                out_own(j, a).start()

        return carry

    lax.fori_loop(0, OWN + 2, step, 0)

    def finish(j, carry):
        for a in range(4):
            half_copy(j, a).wait_send()
            out_own(j, a).wait()
            out_half(j, a).wait_send()
            out_half_in(j, a).wait_recv()
        for copy in key_copies(j) + grad_copies(j):
            copy.wait_send()
        return carry

    lax.fori_loop(0, OWN, finish, 0)


def local(queries, keys, values, grad_out, reach):
    def split(x):
        return x.reshape(FRAMES, ROWS, COLS, HEADS, SIZE).transpose(0, 2, 3, 1, 4)

    def join(x):
        return x.transpose(0, 3, 1, 2, 4).reshape(FRAMES, ROWS, COLS, HEADS * SIZE)

    shape = (FRAMES, COLS, HEADS, ROWS, SIZE)
    anywhere = pl.BlockSpec(memory_space=pl.ANY)
    sems = pltpu.SemaphoreType.DMA
    outs = pl.pallas_call(
        kernel,
        out_shape=[jax.ShapeDtypeStruct(shape, jnp.bfloat16)] * 4,
        in_specs=[pl.BlockSpec(memory_space=pltpu.SMEM)] + [anywhere] * 4,
        out_specs=[anywhere] * 4,
        scratch_shapes=[
            pltpu.VMEM((OWN, 4, 2) + HALF, jnp.bfloat16),
            pltpu.VMEM((OWN, 2, 2, 2) + HALF, jnp.bfloat16),
            pltpu.VMEM((2, 2, TOKENS, SIZE), jnp.float32),
            pltpu.VMEM((OWN, 2, 2, 2) + HALF, jnp.bfloat16),
            pltpu.VMEM((OWN, 2, 2, 2) + HALF, jnp.bfloat16),
            pltpu.VMEM((OWN, 4, 2) + HALF, jnp.bfloat16),
            sems((OWN, 4)), sems((OWN, 4)), sems((OWN, 4)),
            sems((OWN, 2)), sems((OWN, 2)), sems((OWN, 2)), sems((OWN, 2)),
            sems((OWN, 4)), sems((OWN, 4)), sems((OWN, 4)),
        ],
        compiler_params=pltpu.CompilerParams(
            collective_id=0, has_side_effects=True, vmem_limit_bytes=56 << 20
        ),
    )(reach, split(keys), split(values), split(queries), split(grad_out))
    return tuple(join(x) for x in outs)


def solution(mesh):
    spec = P("tm", "height", None, None)
    return jax.shard_map(
        local,
        mesh=mesh,
        in_specs=(spec, spec, spec, spec, P()),
        out_specs=(spec, spec, spec, spec),
        check_vma=False,
    )
```

time: 131 us -> 60.7 us (0.46)
  the two profiles are of different devices: /device:TPU:463 before, /device:TPU:10 now
where the time goes in v1:
time: 60.7 us; the launch traced here: 60.4 us
  Pallas kernels  54.6 us (90%)
  local copies, waits for them, and re-layouts  5.09 us (8%)
  between operations  0.65 us (1%)
    pallas_call x1, Pallas kernels, local(): pl.pallas_call(kernel, out_shape=[jax.ShapeDtypeStruct(shape, jnp.bfloat1...  54.6 us
    unnamed x10, local copies, waits for them, and re-layouts  5.09 us

profile of v1, /device:TPU:10, one launch (start us, length us, event | category | flops | bytes accessed | tf_op | source)
XLA Modules:
  0.0 60.4 jit_solution(13349136239993115221)
XLA Ops:
  0.6 54.6 %shard_map.84 = (bf16[6,6,12,4,128]{4,3,2,1,0:T(4,128)(2,1)}, bf16[6,6,12,4,128]{4,3,2,1,0:T(4,128)(2,1)}, bf16[6,6,12,4,128]{4,3,2,1,0:T(4,128)(2,1)}, bf16[6,6,12,4,128]{4,3,2,1,0:T(4,128)(2,1)}) custom-call(s32[2,12]{1,0:T(2,128)} %reach.1, bf16[6,6,12,4,128]{4,3,2,1,0:T(4,128)(2,1)} %bitcast.24, bf16[6,6,12,4,128]{4,3,2,1,0:T(4,128)(2,1)} %bitcast.25, ...), custom_call_target="tpu_custom_call" | custom-call | tf_op jit(solution)/shard_map/pallas_call | solution.py:209
  55.3 0.0 copy-start.2
  55.3 2.0 %copy.13 = bf16[6,4,6,1536]{3,1,2,0:T(4,128)(2,1)} copy(bf16[6,4,6,1536]{3,1,2,0:T(4,128)(2,1)} %bitcast.31) | data formatting | bytes 884736
  57.3 0.0 copy-done.2
  57.3 0.0 copy-start.1
  57.3 0.8 %copy.14 = bf16[6,4,6,1536]{3,1,2,0:T(4,128)(2,1)} copy(bf16[6,4,6,1536]{3,1,2,0:T(4,128)(2,1)S(1)} %bitcast.30) | data formatting | bytes 884736
  58.0 0.4 copy-done.1
  58.4 0.0 copy-start
  58.4 0.8 %copy.15 = bf16[6,4,6,1536]{3,1,2,0:T(4,128)(2,1)} copy(bf16[6,4,6,1536]{3,1,2,0:T(4,128)(2,1)S(1)} %bitcast.29) | data formatting | bytes 884736
  59.2 0.4 copy-done
  59.6 0.8 %copy.16 = bf16[6,4,6,1536]{3,1,2,0:T(4,128)(2,1)} copy(bf16[6,4,6,1536]{3,1,2,0:T(4,128)(2,1)S(1)} %bitcast.28) | data formatting | bytes 884736
Async XLA Ops:
  55.3 2.0 %copy-start.2 = (bf16[6,6,12,4,128]{4,3,2,1,0:T(4,128)(2,1)S(1)}, bf16[6,6,12,4,128]{4,3,2,1,0:T(4,128)(2,1)}, u32[]{:S(2)}) copy-start(bf16[6,6,12,4,128]{4,3,2,1,0:T(4,128)(2,1)} %get-tuple-element.9) | copy-start | bytes 1327108
  57.3 1.2 %copy-start.1 = (bf16[6,6,12,4,128]{4,3,2,1,0:T(4,128)(2,1)S(1)}, bf16[6,6,12,4,128]{4,3,2,1,0:T(4,128)(2,1)}, u32[]{:S(2)}) copy-start(bf16[6,6,12,4,128]{4,3,2,1,0:T(4,128)(2,1)} %get-tuple-element.10) | copy-start | bytes 1327108
  58.4 1.2 %copy-start = (bf16[6,6,12,4,128]{4,3,2,1,0:T(4,128)(2,1)S(1)}, bf16[6,6,12,4,128]{4,3,2,1,0:T(4,128)(2,1)}, u32[]{:S(2)}) copy-start(bf16[6,6,12,4,128]{4,3,2,1,0:T(4,128)(2,1)} %get-tuple-element.11) | copy-start | bytes 1327108

commit v2 on v1

--- a/solution.py
+++ b/solution.py
@@ -51,7 +51,7 @@
 def kernel(
     reach, k_in, v_in, q_in, d_in, o_out, dq_out, dk_out, dv_out,
     tile, near, local_grad, sent, got, done,
-    own_sem, xs_sem, xr_sem, ks_sem, kr_sem, gs_sem, gr_sem, os_sem, or_sem, ol_sem,
+    own_sem, xs_sem, xr_sem, ks_sem, kr_sem, gs_sem, gr_sem, os_sem, or_sem, ol_sem, hello,
 ):
     tm, height = lax.axis_index("tm"), lax.axis_index("height")
     count = lax.axis_size("tm")
@@ -110,19 +110,55 @@
             done.at[j, a, 1], outputs[a].at[:, :, theirs + j], os_sem.at[j, a], or_sem.at[j, a], partner
         )
 
+    odd = tm % 2
+    seam = (1 - odd) * flip_prev + odd * flip_next
     barrier = pltpu.get_barrier_semaphore()
-    for device in (partner, following, preceding):
-        pl.semaphore_signal(barrier, inc=1, device_id=device, device_id_type=MESH)
-    pl.semaphore_wait(barrier, 3)
-
-    def begin(j, carry):
-        for a in range(4):
-            half_copy(j, a).start()
-        for a in range(4):
-            own_copy(j, a).start()
-        return carry
-
-    lax.fori_loop(0, OWN, begin, 0)
+    pl.semaphore_signal(barrier, inc=1, device_id=partner, device_id_type=MESH)
+
+    @pl.when(odd == 1)
+    def _():
+        pl.semaphore_signal(barrier, inc=1, device_id=preceding, device_id_type=MESH)
+
+    @pl.when((odd == 1) & (seam == 0))
+    def _():
+        pl.semaphore_signal(barrier, inc=1, device_id=following, device_id_type=MESH)
+
+    @pl.when((odd == 0) & (seam == 1))
+    def _():
+        pl.semaphore_signal(barrier, inc=1, device_id=preceding, device_id_type=MESH)
+
+    pl.semaphore_wait(barrier, 3 - 2 * odd + (2 * odd - 1) * seam)
+
+    for first in (0, 2):
+
+        def begin(j, carry, first=first):
+            for a in (first, first + 1):
+                half_copy(j, a).start()
+            for a in (first, first + 1):
+                own_copy(j, a).start()
+            return carry
+
+        lax.fori_loop(0, OWN, begin, 0)
+
+    @pl.when(odd == 0)
+    def _():
+        pl.semaphore_signal(hello.at[0], inc=1, device_id=following, device_id_type=MESH)
+
+    @pl.when((odd == 0) & (seam == 0))
+    def _():
+        pl.semaphore_signal(hello.at[1], inc=1, device_id=preceding, device_id_type=MESH)
+
+    @pl.when((odd == 1) & (seam == 1))
+    def _():
+        pl.semaphore_signal(hello.at[1], inc=1, device_id=following, device_id_type=MESH)
+
+    @pl.when(odd == 1)
+    def _():
+        pl.semaphore_wait(hello.at[0], 1)
+
+    @pl.when(odd != seam)
+    def _():
+        pl.semaphore_wait(hello.at[1], 1)
 
     def flat(x):
         return x.reshape(TOKENS, SIZE)
@@ -130,58 +166,59 @@
     def tiled(x):
         return x.astype(jnp.bfloat16).reshape((2,) + HALF)
 
-    def step(it, carry):
-        @pl.when(it < OWN)
-        def _():
-            j = it
-            for a in range(4):
-                own_copy(j, a).wait()
-                half_copy(j, a).wait_recv()
-            for copy in key_copies(j):
-                copy.start()
-
-        @pl.when((it >= 1) & (it < OWN + 1))
-        def _():
-            j = it - 1
-            for copy in key_copies(j):
-                copy.wait_recv()
-            k, v, q, d = [flat(tile[j, a]) for a in range(4)]
-            ks = [k, flat(near[j, 0, 0]), flat(near[j, 1, 0])]
-            vs = [v, flat(near[j, 0, 1]), flat(near[j, 1, 1])]
-            back = (reach[0, mine + j] >= 1) & (tm >= 1)
-            ahead = (reach[1, mine + j] >= 1) & (tm < count - 1)
-            biases = [None, jnp.where(back, 0.0, -1e30), jnp.where(ahead, 0.0, -1e30)]
-            attended, grad_query, key_parts, value_parts = one_head(q, d, ks, vs, biases)
-            done[j, 0] = tiled(attended)
-            done[j, 1] = tiled(grad_query)
-            local_grad[j % 2, 0] = key_parts[0]
-            local_grad[j % 2, 1] = value_parts[0]
+    def arrived(j, first):
+        for a in (first, first + 1):
+            own_copy(j, a).wait()
+            half_copy(j, a).wait_recv()
+
+    def forward(j, carry):
+        arrived(j, 0)
+        for copy in key_copies(j):
+            copy.start()
+        return carry
+
+    lax.fori_loop(0, OWN, forward, 0)
+
+    def compute(j, carry):
+        arrived(j, 2)
+        for copy in key_copies(j):
+            copy.wait_recv()
+        k, v, q, d = [flat(tile[j, a]) for a in range(4)]
+        ks = [k, flat(near[j, 0, 0]), flat(near[j, 1, 0])]
+        vs = [v, flat(near[j, 0, 1]), flat(near[j, 1, 1])]
+        back = (reach[0, mine + j] >= 1) & (tm >= 1)
+        ahead = (reach[1, mine + j] >= 1) & (tm < count - 1)
+        biases = [None, jnp.where(back, 0.0, -1e30), jnp.where(ahead, 0.0, -1e30)]
+        attended, grad_query, key_parts, value_parts = one_head(q, d, ks, vs, biases)
+        for way in range(2):
+            sent[j, way, 0] = tiled(key_parts[1 + way])
+            sent[j, way, 1] = tiled(value_parts[1 + way])
+        for copy in grad_copies(j):
+            copy.start()
+        done[j, 0] = tiled(attended)
+        done[j, 1] = tiled(grad_query)
+        for a in range(2):
+            out_half(j, a).start()
+            out_own(j, a).start()
+        local_grad[j, 0] = key_parts[0]
+        local_grad[j, 1] = value_parts[0]
+        return carry
+
+    lax.fori_loop(0, OWN, compute, 0)
+
+    def gather(j, carry):
+        for copy in grad_copies(j):
+            copy.wait_recv()
+        for part in range(2):
+            total = local_grad[j, part]
             for way in range(2):
-                sent[j, way, 0] = tiled(key_parts[1 + way])
-                sent[j, way, 1] = tiled(value_parts[1 + way])
-            for copy in grad_copies(j):
-                copy.start()
-            for a in range(2):
-                out_half(j, a).start()
-                out_own(j, a).start()
-
-        @pl.when(it >= 2)
-        def _():
-            j = it - 2
-            for copy in grad_copies(j):
-                copy.wait_recv()
-            for part in range(2):
-                total = local_grad[j % 2, part]
-                for way in range(2):
-                    total = total + flat(got[j, way, part]).astype(jnp.float32)
-                done[j, 2 + part] = tiled(total)
-            for a in range(2, 4):
-                out_half(j, a).start()
-                out_own(j, a).start()
-
-        return carry
-
-    lax.fori_loop(0, OWN + 2, step, 0)
+                total = total + flat(got[j, way, part]).astype(jnp.float32)
+            done[j, 2 + part] = tiled(total)
+            out_half(j, 2 + part).start()
+            out_own(j, 2 + part).start()
+        return carry
+
+    lax.fori_loop(0, OWN, gather, 0)
 
     def finish(j, carry):
         for a in range(4):
@@ -214,13 +251,14 @@
         scratch_shapes=[
             pltpu.VMEM((OWN, 4, 2) + HALF, jnp.bfloat16),
             pltpu.VMEM((OWN, 2, 2, 2) + HALF, jnp.bfloat16),
-            pltpu.VMEM((2, 2, TOKENS, SIZE), jnp.float32),
+            pltpu.VMEM((OWN, 2, TOKENS, SIZE), jnp.float32),
             pltpu.VMEM((OWN, 2, 2, 2) + HALF, jnp.bfloat16),
             pltpu.VMEM((OWN, 2, 2, 2) + HALF, jnp.bfloat16),
             pltpu.VMEM((OWN, 4, 2) + HALF, jnp.bfloat16),
             sems((OWN, 4)), sems((OWN, 4)), sems((OWN, 4)),
             sems((OWN, 2)), sems((OWN, 2)), sems((OWN, 2)), sems((OWN, 2)),
             sems((OWN, 4)), sems((OWN, 4)), sems((OWN, 4)),
+            pltpu.SemaphoreType.REGULAR((2,)),
         ],
         compiler_params=pltpu.CompilerParams(
             collective_id=0, has_side_effects=True, vmem_limit_bytes=56 << 20

time: 60.7 us -> 49.9 us (0.82)
  the two profiles are of different devices: /device:TPU:10 before, /device:TPU:24 now
where the time goes in v2:
time: 49.9 us; the launch traced here: 49.6 us
  Pallas kernels  43.8 us (88%)
  local copies, waits for them, and re-layouts  5.09 us (10%)
  between operations  0.65 us (1%)
    pallas_call x1, Pallas kernels, local(): pl.pallas_call(kernel, out_shape=[jax.ShapeDtypeStruct(shape, jnp.bfloat1...  43.8 us
    unnamed x10, local copies, waits for them, and re-layouts  5.09 us

profile of v2, /device:TPU:24, one launch (start us, length us, event | category | flops | bytes accessed | tf_op | source)
XLA Modules:
  0.0 49.6 jit_solution(5871884980563728141)
XLA Ops:
  0.6 43.8 %shard_map.84 = (bf16[6,6,12,4,128]{4,3,2,1,0:T(4,128)(2,1)}, bf16[6,6,12,4,128]{4,3,2,1,0:T(4,128)(2,1)}, bf16[6,6,12,4,128]{4,3,2,1,0:T(4,128)(2,1)}, bf16[6,6,12,4,128]{4,3,2,1,0:T(4,128)(2,1)}) custom-call(s32[2,12]{1,0:T(2,128)} %reach.1, bf16[6,6,12,4,128]{4,3,2,1,0:T(4,128)(2,1)} %bitcast.24, bf16[6,6,12,4,128]{4,3,2,1,0:T(4,128)(2,1)} %bitcast.25, ...), custom_call_target="tpu_custom_call" | custom-call | tf_op jit(solution)/shard_map/pallas_call | solution.py:246
  44.5 0.0 copy-start.2
  44.5 2.0 %copy.13 = bf16[6,4,6,1536]{3,1,2,0:T(4,128)(2,1)} copy(bf16[6,4,6,1536]{3,1,2,0:T(4,128)(2,1)} %bitcast.31) | data formatting | bytes 884736
  46.5 0.0 copy-done.2
  46.5 0.0 copy-start.1
  46.5 0.8 %copy.14 = bf16[6,4,6,1536]{3,1,2,0:T(4,128)(2,1)} copy(bf16[6,4,6,1536]{3,1,2,0:T(4,128)(2,1)S(1)} %bitcast.30) | data formatting | bytes 884736
  47.2 0.4 copy-done.1
  47.6 0.0 copy-start
  47.6 0.8 %copy.15 = bf16[6,4,6,1536]{3,1,2,0:T(4,128)(2,1)} copy(bf16[6,4,6,1536]{3,1,2,0:T(4,128)(2,1)S(1)} %bitcast.29) | data formatting | bytes 884736
  48.4 0.4 copy-done
  48.8 0.8 %copy.16 = bf16[6,4,6,1536]{3,1,2,0:T(4,128)(2,1)} copy(bf16[6,4,6,1536]{3,1,2,0:T(4,128)(2,1)S(1)} %bitcast.28) | data formatting | bytes 884736
Async XLA Ops:
  44.5 2.0 %copy-start.2 = (bf16[6,6,12,4,128]{4,3,2,1,0:T(4,128)(2,1)S(1)}, bf16[6,6,12,4,128]{4,3,2,1,0:T(4,128)(2,1)}, u32[]{:S(2)}) copy-start(bf16[6,6,12,4,128]{4,3,2,1,0:T(4,128)(2,1)} %get-tuple-element.9) | copy-start | bytes 1327108
  46.5 1.2 %copy-start.1 = (bf16[6,6,12,4,128]{4,3,2,1,0:T(4,128)(2,1)S(1)}, bf16[6,6,12,4,128]{4,3,2,1,0:T(4,128)(2,1)}, u32[]{:S(2)}) copy-start(bf16[6,6,12,4,128]{4,3,2,1,0:T(4,128)(2,1)} %get-tuple-element.10) | copy-start | bytes 1327108
  47.6 1.2 %copy-start = (bf16[6,6,12,4,128]{4,3,2,1,0:T(4,128)(2,1)S(1)}, bf16[6,6,12,4,128]{4,3,2,1,0:T(4,128)(2,1)}, u32[]{:S(2)}) copy-start(bf16[6,6,12,4,128]{4,3,2,1,0:T(4,128)(2,1)} %get-tuple-element.11) | copy-start | bytes 1327108

commit v3 on v2

--- a/solution.py
+++ b/solution.py
@@ -49,8 +49,8 @@
 
 
 def kernel(
-    reach, k_in, v_in, q_in, d_in, o_out, dq_out, dk_out, dv_out,
-    tile, near, local_grad, sent, got, done,
+    reach_in, k_in, v_in, q_in, d_in, o_out, dq_out, dk_out, dv_out,
+    reach, tile, near, local_grad, sent, got, done, reach_sem,
     own_sem, xs_sem, xr_sem, ks_sem, kr_sem, gs_sem, gr_sem, os_sem, or_sem, ol_sem, hello,
 ):
     tm, height = lax.axis_index("tm"), lax.axis_index("height")
@@ -110,6 +110,8 @@
             done.at[j, a, 1], outputs[a].at[:, :, theirs + j], os_sem.at[j, a], or_sem.at[j, a], partner
         )
 
+    reach_copy = pltpu.make_async_copy(reach_in, reach, reach_sem)
+    reach_copy.start()
     odd = tm % 2
     seam = (1 - odd) * flip_prev + odd * flip_next
     barrier = pltpu.get_barrier_semaphore()
@@ -204,6 +206,7 @@
         local_grad[j, 1] = value_parts[0]
         return carry
 
+    reach_copy.wait()
     lax.fori_loop(0, OWN, compute, 0)
 
     def gather(j, carry):
@@ -233,6 +236,15 @@
     lax.fori_loop(0, OWN, finish, 0)
 
 
+def deliver(*refs):
+    got, outs, sem = refs[:4], refs[4:8], refs[8]
+    copies = [pltpu.make_async_copy(g, o, sem.at[i]) for i, (g, o) in enumerate(zip(got, outs))]
+    for copy in copies:
+        copy.start()
+    for copy in copies:
+        copy.wait()
+
+
 def local(queries, keys, values, grad_out, reach):
     def split(x):
         return x.reshape(FRAMES, ROWS, COLS, HEADS, SIZE).transpose(0, 2, 3, 1, 4)
@@ -243,27 +255,38 @@
     shape = (FRAMES, COLS, HEADS, ROWS, SIZE)
     anywhere = pl.BlockSpec(memory_space=pl.ANY)
     sems = pltpu.SemaphoreType.DMA
+    held = (reach, split(keys), split(values), split(queries), split(grad_out))
     outs = pl.pallas_call(
         kernel,
         out_shape=[jax.ShapeDtypeStruct(shape, jnp.bfloat16)] * 4,
-        in_specs=[pl.BlockSpec(memory_space=pltpu.SMEM)] + [anywhere] * 4,
+        in_specs=[pl.BlockSpec(memory_space=pltpu.HBM)] * 5,
         out_specs=[anywhere] * 4,
         scratch_shapes=[
+            pltpu.SMEM((2, HEADS), jnp.int32),
             pltpu.VMEM((OWN, 4, 2) + HALF, jnp.bfloat16),
             pltpu.VMEM((OWN, 2, 2, 2) + HALF, jnp.bfloat16),
             pltpu.VMEM((OWN, 2, TOKENS, SIZE), jnp.float32),
             pltpu.VMEM((OWN, 2, 2, 2) + HALF, jnp.bfloat16),
             pltpu.VMEM((OWN, 2, 2, 2) + HALF, jnp.bfloat16),
             pltpu.VMEM((OWN, 4, 2) + HALF, jnp.bfloat16),
+            sems,
             sems((OWN, 4)), sems((OWN, 4)), sems((OWN, 4)),
             sems((OWN, 2)), sems((OWN, 2)), sems((OWN, 2)), sems((OWN, 2)),
             sems((OWN, 4)), sems((OWN, 4)), sems((OWN, 4)),
             pltpu.SemaphoreType.REGULAR((2,)),
         ],
         compiler_params=pltpu.CompilerParams(
-            collective_id=0, has_side_effects=True, vmem_limit_bytes=56 << 20
+            collective_id=0, has_side_effects=True, vmem_limit_bytes=24 << 20
         ),
-    )(reach, split(keys), split(values), split(queries), split(grad_out))
+    )(*[pltpu.with_memory_space_constraint(x, pltpu.HBM) for x in held])
+    outs = pl.pallas_call(
+        deliver,
+        out_shape=[jax.ShapeDtypeStruct(shape, jnp.bfloat16)] * 4,
+        in_specs=[anywhere] * 4,
+        out_specs=[pl.BlockSpec(memory_space=pltpu.HBM)] * 4,
+        scratch_shapes=[sems((4,))],
+        compiler_params=pltpu.CompilerParams(vmem_limit_bytes=2 << 20),
+    )(*outs)
     return tuple(join(x) for x in outs)
 
 

time: 49.9 us -> 45.1 us (0.904)
  local copies, waits for them, and re-layouts: 5.09 us -> 0 us
  Pallas kernels: 43.8 us -> 44.3 us
    unnamed x10 -> x0, local copies, waits for them, and re-layouts: 5.09 us -> none
    pallas_call x0 -> x1, Pallas kernels: none -> 1.24 us  [local(): pl.pallas_call(deliver, out_shape=[jax.ShapeDtypeStruct(shape, jnp.bfloat...]
    pallas_call x1, Pallas kernels: 43.8 us -> 43 us  [local(): pl.pallas_call(kernel, out_shape=[jax.ShapeDtypeStruct(shape, jnp.bfloat1...]
where the time goes in v3:
time: 45.1 us; the launch traced here: 44.9 us
  Pallas kernels  44.3 us (98%)
  between operations  0.64 us (1%)
    pallas_call x1, Pallas kernels, local(): pl.pallas_call(kernel, out_shape=[jax.ShapeDtypeStruct(shape, jnp.bfloat1...  43 us
    pallas_call x1, Pallas kernels, local(): pl.pallas_call(deliver, out_shape=[jax.ShapeDtypeStruct(shape, jnp.bfloat...  1.24 us

profile of v3, /device:TPU:24, one launch (start us, length us, event | category | flops | bytes accessed | tf_op | source)
XLA Modules:
  0.0 44.9 jit_solution(3615381865453467135)
XLA Ops:
  0.6 43.0 %shard_map.84 = (bf16[6,6,12,4,128]{4,3,2,1,0:T(4,128)(2,1)S(1)}, bf16[6,6,12,4,128]{4,3,2,1,0:T(4,128)(2,1)S(1)}, bf16[6,6,12,4,128]{4,3,2,1,0:T(4,128)(2,1)S(1)}, bf16[6,6,12,4,128]{4,3,2,1,0:T(4,128)(2,1)S(1)}) custom-call(s32[2,12]{1,0:T(2,128)} %reach_in.1, bf16[6,6,12,4,128]{4,3,2,1,0:T(4,128)(2,1)} %bitcast.24, bf16[6,6,12,4,128]{4,3,2,1,0:T(4,128)(2,1)} %bitcast.25, ...), custom_call_target="tpu_custom_call" | custom-call | tf_op jit(solution)/shard_map/pallas_call | solution.py:259
  43.7 1.2 %shard_map.85 = (bf16[6,6,12,4,128]{4,3,2,1,0:T(4,128)(2,1)}, bf16[6,6,12,4,128]{4,3,2,1,0:T(4,128)(2,1)}, bf16[6,6,12,4,128]{4,3,2,1,0:T(4,128)(2,1)}, bf16[6,6,12,4,128]{4,3,2,1,0:T(4,128)(2,1)}) custom-call(bf16[6,6,12,4,128]{4,3,2,1,0:T(4,128)(2,1)S(1)} %get-tuple-element.12.refs_0_, bf16[6,6,12,4,128]{4,3,2,1,0:T(4,128)(2,1)S(1)} %get-tuple-element.13.refs_1_, ...), custom_call_target="tpu_custom_call" | custom-call | tf_op jit(solution)/shard_map/pallas_call | solution.py:282

commit v4 on v3

--- a/solution.py
+++ b/solution.py
@@ -68,7 +68,7 @@
 
     def own_copy(j, a):
         return pltpu.make_async_copy(
-            inputs[a].at[:, :, mine + j], tile.at[j, a, 0], own_sem.at[j, a]
+            inputs[a].at[:, :, mine + j], tile.at[j, a, 0], own_sem.at[a // 2]
         )
 
     def remote(src, dst, send, recv, device):
@@ -79,35 +79,30 @@
 
     def half_copy(j, a):
         return remote(
-            inputs[a].at[:, :, theirs + j], tile.at[j, a, 1], xs_sem.at[j, a], xr_sem.at[j, a], partner
+            inputs[a].at[:, :, theirs + j], tile.at[j, a, 1], xs_sem, xr_sem.at[j, a // 2], partner
         )
 
     def key_copies(j):
         block = tile.at[j, pl.ds(0, 2)]
         return (
-            remote(block, near.at[j, 0], ks_sem.at[j, 0], kr_sem.at[j, 0], following),
-            remote(block, near.at[j, 1], ks_sem.at[j, 1], kr_sem.at[j, 1], preceding),
+            remote(block, near.at[j, 0], ks_sem, kr_sem.at[j], following),
+            remote(block, near.at[j, 1], ks_sem, kr_sem.at[j], preceding),
         )
 
     def grad_copies(j):
         return (
-            remote(sent.at[j, 1], got.at[j, 0], gs_sem.at[j, 0], gr_sem.at[j, 0], following),
-            remote(sent.at[j, 0], got.at[j, 1], gs_sem.at[j, 1], gr_sem.at[j, 1], preceding),
+            remote(sent.at[j, 1], got.at[j, 0], gs_sem, gr_sem.at[j], following),
+            remote(sent.at[j, 0], got.at[j, 1], gs_sem, gr_sem.at[j], preceding),
         )
 
     def out_own(j, a):
         return pltpu.make_async_copy(
-            done.at[j, a, 0], outputs[a].at[:, :, mine + j], ol_sem.at[j, a]
+            done.at[j, a, 0], outputs[a].at[:, :, mine + j], ol_sem
         )
 
     def out_half(j, a):
         return remote(
-            done.at[j, a, 1], outputs[a].at[:, :, mine + j], os_sem.at[j, a], or_sem.at[j, a], partner
-        )
-
-    def out_half_in(j, a):
-        return remote(
-            done.at[j, a, 1], outputs[a].at[:, :, theirs + j], os_sem.at[j, a], or_sem.at[j, a], partner
+            done.at[j, a, 1], outputs[a].at[:, :, mine + j], os_sem, or_sem, partner
         )
 
     reach_copy = pltpu.make_async_copy(reach_in, reach, reach_sem)
@@ -168,10 +163,15 @@
     def tiled(x):
         return x.astype(jnp.bfloat16).reshape((2,) + HALF)
 
-    def arrived(j, first):
-        for a in (first, first + 1):
-            own_copy(j, a).wait()
-            half_copy(j, a).wait_recv()
+    def arrived(j, pair):
+        halves = tile.at[j, pl.ds(2 * pair, 2)]
+        remote(halves.at[:, 0], halves.at[:, 1], xs_sem, xr_sem.at[j, pair], partner).wait_recv()
+
+    def own_arrived(pair):
+        halves = tile.at[:, pl.ds(2 * pair, 2)]
+        pltpu.make_async_copy(halves.at[:, :, 1], halves.at[:, :, 0], own_sem.at[pair]).wait()
+
+    own_arrived(0)
 
     def forward(j, carry):
         arrived(j, 0)
@@ -182,9 +182,8 @@
     lax.fori_loop(0, OWN, forward, 0)
 
     def compute(j, carry):
-        arrived(j, 2)
-        for copy in key_copies(j):
-            copy.wait_recv()
+        arrived(j, 1)
+        remote(sent.at[j], near.at[j], ks_sem, kr_sem.at[j], partner).wait_recv()
         k, v, q, d = [flat(tile[j, a]) for a in range(4)]
         ks = [k, flat(near[j, 0, 0]), flat(near[j, 1, 0])]
         vs = [v, flat(near[j, 0, 1]), flat(near[j, 1, 1])]
@@ -206,12 +205,12 @@
         local_grad[j, 1] = value_parts[0]
         return carry
 
+    own_arrived(1)
     reach_copy.wait()
     lax.fori_loop(0, OWN, compute, 0)
 
     def gather(j, carry):
-        for copy in grad_copies(j):
-            copy.wait_recv()
+        remote(sent.at[j], got.at[j], gs_sem, gr_sem.at[j], partner).wait_recv()
         for part in range(2):
             total = local_grad[j, part]
             for way in range(2):
@@ -223,17 +222,11 @@
 
     lax.fori_loop(0, OWN, gather, 0)
 
-    def finish(j, carry):
-        for a in range(4):
-            half_copy(j, a).wait_send()
-            out_own(j, a).wait()
-            out_half(j, a).wait_send()
-            out_half_in(j, a).wait_recv()
-        for copy in key_copies(j) + grad_copies(j):
-            copy.wait_send()
-        return carry
-
-    lax.fori_loop(0, OWN, finish, 0)
+    remote(tile.at[:, :, 0], tile.at[:, :, 1], xs_sem, xr_sem.at[0, 0], partner).wait_send()
+    remote(near, got, ks_sem, kr_sem.at[0], partner).wait_send()
+    remote(sent, got, gs_sem, gr_sem.at[0], partner).wait_send()
+    pltpu.make_async_copy(done.at[:, :, 0], done.at[:, :, 1], ol_sem).wait()
+    remote(done.at[:, :, 1], done.at[:, :, 0], os_sem, or_sem, partner).wait()
 
 
 def deliver(*refs):
@@ -270,9 +263,9 @@
             pltpu.VMEM((OWN, 2, 2, 2) + HALF, jnp.bfloat16),
             pltpu.VMEM((OWN, 4, 2) + HALF, jnp.bfloat16),
             sems,
-            sems((OWN, 4)), sems((OWN, 4)), sems((OWN, 4)),
-            sems((OWN, 2)), sems((OWN, 2)), sems((OWN, 2)), sems((OWN, 2)),
-            sems((OWN, 4)), sems((OWN, 4)), sems((OWN, 4)),
+            sems((2,)), sems, sems((OWN, 2)),
+            sems, sems((OWN,)), sems, sems((OWN,)),
+            sems, sems, sems,
             pltpu.SemaphoreType.REGULAR((2,)),
         ],
         compiler_params=pltpu.CompilerParams(

time: 45.1 us -> 43.7 us (0.969)
  Pallas kernels: 44.3 us -> 42.8 us
    pallas_call x1, Pallas kernels: 43 us -> 41.6 us  [local(): pl.pallas_call(kernel, out_shape=[jax.ShapeDtypeStruct(shape, jnp.bfloat1...]
where the time goes in v4:
time: 43.7 us; the launch traced here: 43.5 us
  Pallas kernels  42.8 us (98%)
  between operations  0.64 us (1%)
    pallas_call x1, Pallas kernels, local(): pl.pallas_call(kernel, out_shape=[jax.ShapeDtypeStruct(shape, jnp.bfloat1...  41.6 us
    pallas_call x1, Pallas kernels, local(): pl.pallas_call(deliver, out_shape=[jax.ShapeDtypeStruct(shape, jnp.bfloat...  1.24 us

profile of v4, /device:TPU:24, one launch (start us, length us, event | category | flops | bytes accessed | tf_op | source)
XLA Modules:
  0.0 43.5 jit_solution(11496841683585673949)
XLA Ops:
  0.6 41.6 %shard_map.84 = (bf16[6,6,12,4,128]{4,3,2,1,0:T(4,128)(2,1)S(1)}, bf16[6,6,12,4,128]{4,3,2,1,0:T(4,128)(2,1)S(1)}, bf16[6,6,12,4,128]{4,3,2,1,0:T(4,128)(2,1)S(1)}, bf16[6,6,12,4,128]{4,3,2,1,0:T(4,128)(2,1)S(1)}) custom-call(s32[2,12]{1,0:T(2,128)} %reach_in.1, bf16[6,6,12,4,128]{4,3,2,1,0:T(4,128)(2,1)} %bitcast.24, bf16[6,6,12,4,128]{4,3,2,1,0:T(4,128)(2,1)} %bitcast.25, ...), custom_call_target="tpu_custom_call" | custom-call | tf_op jit(solution)/shard_map/pallas_call | solution.py:252
  42.2 1.2 %shard_map.85 = (bf16[6,6,12,4,128]{4,3,2,1,0:T(4,128)(2,1)}, bf16[6,6,12,4,128]{4,3,2,1,0:T(4,128)(2,1)}, bf16[6,6,12,4,128]{4,3,2,1,0:T(4,128)(2,1)}, bf16[6,6,12,4,128]{4,3,2,1,0:T(4,128)(2,1)}) custom-call(bf16[6,6,12,4,128]{4,3,2,1,0:T(4,128)(2,1)S(1)} %get-tuple-element.12.refs_0_, bf16[6,6,12,4,128]{4,3,2,1,0:T(4,128)(2,1)S(1)} %get-tuple-element.13.refs_1_, ...), custom_call_target="tpu_custom_call" | custom-call | tf_op jit(solution)/shard_map/pallas_call | solution.py:275

commit v5 on v4

--- a/solution.py
+++ b/solution.py
@@ -17,6 +17,7 @@
 FACTOR = SIZE**-0.5
 FACTOR2 = FACTOR * math.log2(math.e)
 RING = 32
+EARLY = 4
 
 
 def dot(a, b, over_a, over_b):
@@ -79,20 +80,20 @@
 
     def half_copy(j, a):
         return remote(
-            inputs[a].at[:, :, theirs + j], tile.at[j, a, 1], xs_sem, xr_sem.at[j, a // 2], partner
+            inputs[a].at[:, :, theirs + j], tile.at[j, a, 1], xs_sem, xr_sem.at[j // 2, a // 2], partner
         )
 
     def key_copies(j):
         block = tile.at[j, pl.ds(0, 2)]
         return (
-            remote(block, near.at[j, 0], ks_sem, kr_sem.at[j], following),
-            remote(block, near.at[j, 1], ks_sem, kr_sem.at[j], preceding),
+            remote(block, near.at[j, 0], ks_sem, kr_sem.at[j // 2], following),
+            remote(block, near.at[j, 1], ks_sem, kr_sem.at[j // 2], preceding),
         )
 
     def grad_copies(j):
         return (
-            remote(sent.at[j, 1], got.at[j, 0], gs_sem, gr_sem.at[j], following),
-            remote(sent.at[j, 0], got.at[j, 1], gs_sem, gr_sem.at[j], preceding),
+            remote(sent.at[j, 1], got.at[j, 0], gs_sem, gr_sem.at[j // 2], following),
+            remote(sent.at[j, 0], got.at[j, 1], gs_sem, gr_sem.at[j // 2], preceding),
         )
 
     def out_own(j, a):
@@ -100,17 +101,16 @@
             done.at[j, a, 0], outputs[a].at[:, :, mine + j], ol_sem
         )
 
-    def out_half(j, a):
+    def out_half(j, a, late=0):
         return remote(
-            done.at[j, a, 1], outputs[a].at[:, :, mine + j], os_sem, or_sem, partner
-        )
-
+            done.at[j, a, 1], outputs[a].at[:, :, mine + j], os_sem.at[late], or_sem, partner
+        )
+
+    barrier = pltpu.get_barrier_semaphore()
+    pl.semaphore_signal(barrier, inc=1, device_id=partner, device_id_type=MESH)
     reach_copy = pltpu.make_async_copy(reach_in, reach, reach_sem)
-    reach_copy.start()
     odd = tm % 2
     seam = (1 - odd) * flip_prev + odd * flip_next
-    barrier = pltpu.get_barrier_semaphore()
-    pl.semaphore_signal(barrier, inc=1, device_id=partner, device_id_type=MESH)
 
     @pl.when(odd == 1)
     def _():
@@ -137,6 +137,8 @@
 
         lax.fori_loop(0, OWN, begin, 0)
 
+    reach_copy.start()
+
     @pl.when(odd == 0)
     def _():
         pl.semaphore_signal(hello.at[0], inc=1, device_id=following, device_id_type=MESH)
@@ -164,8 +166,12 @@
         return x.astype(jnp.bfloat16).reshape((2,) + HALF)
 
     def arrived(j, pair):
-        halves = tile.at[j, pl.ds(2 * pair, 2)]
-        remote(halves.at[:, 0], halves.at[:, 1], xs_sem, xr_sem.at[j, pair], partner).wait_recv()
+        @pl.when(j % 2 == 0)
+        def _():
+            halves = tile.at[pl.ds(j, 2), pl.ds(2 * pair, 2)]
+            remote(
+                halves.at[:, :, 0], halves.at[:, :, 1], xs_sem, xr_sem.at[j // 2, pair], partner
+            ).wait_recv()
 
     def own_arrived(pair):
         halves = tile.at[:, pl.ds(2 * pair, 2)]
@@ -183,7 +189,12 @@
 
     def compute(j, carry):
         arrived(j, 1)
-        remote(sent.at[j], near.at[j], ks_sem, kr_sem.at[j], partner).wait_recv()
+
+        @pl.when(j % 2 == 0)
+        def _():
+            two = pl.ds(j, 2)
+            remote(sent.at[two], near.at[two], ks_sem, kr_sem.at[j // 2], partner).wait_recv()
+
         k, v, q, d = [flat(tile[j, a]) for a in range(4)]
         ks = [k, flat(near[j, 0, 0]), flat(near[j, 1, 0])]
         vs = [v, flat(near[j, 0, 1]), flat(near[j, 1, 1])]
@@ -209,14 +220,28 @@
     reach_copy.wait()
     lax.fori_loop(0, OWN, compute, 0)
 
+    def early_left():
+        first = done.at[pl.ds(0, EARLY), pl.ds(2, 2)]
+        remote(first.at[:, :, 0], first.at[:, :, 1], os_sem.at[1], or_sem, partner).wait_send()
+
     def gather(j, carry):
-        remote(sent.at[j], got.at[j], gs_sem, gr_sem.at[j], partner).wait_recv()
+        late = 1 + j // EARLY
+
+        @pl.when((j == EARLY) & (odd == 1))
+        def _():
+            early_left()
+
+        @pl.when(j % 2 == 0)
+        def _():
+            two = pl.ds(j, 2)
+            remote(sent.at[two], got.at[two], gs_sem, gr_sem.at[j // 2], partner).wait_recv()
+
         for part in range(2):
             total = local_grad[j, part]
             for way in range(2):
                 total = total + flat(got[j, way, part]).astype(jnp.float32)
             done[j, 2 + part] = tiled(total)
-            out_half(j, 2 + part).start()
+            out_half(j, 2 + part, late).start()
             out_own(j, 2 + part).start()
         return carry
 
@@ -226,7 +251,16 @@
     remote(near, got, ks_sem, kr_sem.at[0], partner).wait_send()
     remote(sent, got, gs_sem, gr_sem.at[0], partner).wait_send()
     pltpu.make_async_copy(done.at[:, :, 0], done.at[:, :, 1], ol_sem).wait()
-    remote(done.at[:, :, 1], done.at[:, :, 0], os_sem, or_sem, partner).wait()
+
+    @pl.when(odd == 0)
+    def _():
+        early_left()
+
+    both = done.at[:, pl.ds(0, 2)]
+    last = done.at[pl.ds(EARLY, OWN - EARLY), pl.ds(2, 2)]
+    remote(both.at[:, :, 0], both.at[:, :, 1], os_sem.at[0], or_sem, partner).wait_send()
+    remote(last.at[:, :, 0], last.at[:, :, 1], os_sem.at[2], or_sem, partner).wait_send()
+    remote(done.at[:, :, 1], done.at[:, :, 0], os_sem.at[0], or_sem, partner).wait_recv()
 
 
 def deliver(*refs):
@@ -263,9 +297,9 @@
             pltpu.VMEM((OWN, 2, 2, 2) + HALF, jnp.bfloat16),
             pltpu.VMEM((OWN, 4, 2) + HALF, jnp.bfloat16),
             sems,
-            sems((2,)), sems, sems((OWN, 2)),
-            sems, sems((OWN,)), sems, sems((OWN,)),
-            sems, sems, sems,
+            sems((2,)), sems, sems((OWN // 2, 2)),
+            sems, sems((OWN // 2,)), sems, sems((OWN // 2,)),
+            sems((3,)), sems, sems,
             pltpu.SemaphoreType.REGULAR((2,)),
         ],
         compiler_params=pltpu.CompilerParams(

time: 43.7 us -> 45.7 us (1.046)
  Pallas kernels: 42.8 us -> 44.5 us
    pallas_call x1, Pallas kernels: 41.6 us -> 43.3 us  [local(): pl.pallas_call(kernel, out_shape=[jax.ShapeDtypeStruct(shape, jnp.bfloat1...]
where the time goes in v5:
time: 45.7 us; the launch traced here: 45.1 us
  Pallas kernels  44.5 us (97%)
  between operations  0.64 us (1%)
    pallas_call x1, Pallas kernels, local(): pl.pallas_call(kernel, out_shape=[jax.ShapeDtypeStruct(shape, jnp.bfloat1...  43.3 us
    pallas_call x1, Pallas kernels, local(): pl.pallas_call(deliver, out_shape=[jax.ShapeDtypeStruct(shape, jnp.bfloat...  1.24 us

profile of v5, /device:TPU:24, one launch (start us, length us, event | category | flops | bytes accessed | tf_op | source)
XLA Modules:
  0.0 45.1 jit_solution(16747693402319205275)
XLA Ops:
  0.6 43.3 %shard_map.84 = (bf16[6,6,12,4,128]{4,3,2,1,0:T(4,128)(2,1)S(1)}, bf16[6,6,12,4,128]{4,3,2,1,0:T(4,128)(2,1)S(1)}, bf16[6,6,12,4,128]{4,3,2,1,0:T(4,128)(2,1)S(1)}, bf16[6,6,12,4,128]{4,3,2,1,0:T(4,128)(2,1)S(1)}) custom-call(s32[2,12]{1,0:T(2,128)} %reach_in.1, bf16[6,6,12,4,128]{4,3,2,1,0:T(4,128)(2,1)} %bitcast.24, bf16[6,6,12,4,128]{4,3,2,1,0:T(4,128)(2,1)} %bitcast.25, ...), custom_call_target="tpu_custom_call" | custom-call | tf_op jit(solution)/shard_map/pallas_call | solution.py:286
  43.9 1.2 %shard_map.85 = (bf16[6,6,12,4,128]{4,3,2,1,0:T(4,128)(2,1)}, bf16[6,6,12,4,128]{4,3,2,1,0:T(4,128)(2,1)}, bf16[6,6,12,4,128]{4,3,2,1,0:T(4,128)(2,1)}, bf16[6,6,12,4,128]{4,3,2,1,0:T(4,128)(2,1)}) custom-call(bf16[6,6,12,4,128]{4,3,2,1,0:T(4,128)(2,1)S(1)} %get-tuple-element.12.refs_0_, bf16[6,6,12,4,128]{4,3,2,1,0:T(4,128)(2,1)S(1)} %get-tuple-element.13.refs_1_, ...), custom_call_target="tpu_custom_call" | custom-call | tf_op jit(solution)/shard_map/pallas_call | solution.py:309

commit v6 on v4

--- a/solution.py
+++ b/solution.py
@@ -17,6 +17,7 @@
 FACTOR = SIZE**-0.5
 FACTOR2 = FACTOR * math.log2(math.e)
 RING = 32
+EARLY = 4
 
 
 def dot(a, b, over_a, over_b):
@@ -100,17 +101,16 @@
             done.at[j, a, 0], outputs[a].at[:, :, mine + j], ol_sem
         )
 
-    def out_half(j, a):
+    def out_half(j, a, late=0):
         return remote(
-            done.at[j, a, 1], outputs[a].at[:, :, mine + j], os_sem, or_sem, partner
-        )
-
+            done.at[j, a, 1], outputs[a].at[:, :, mine + j], os_sem.at[late], or_sem, partner
+        )
+
+    barrier = pltpu.get_barrier_semaphore()
+    pl.semaphore_signal(barrier, inc=1, device_id=partner, device_id_type=MESH)
     reach_copy = pltpu.make_async_copy(reach_in, reach, reach_sem)
-    reach_copy.start()
     odd = tm % 2
     seam = (1 - odd) * flip_prev + odd * flip_next
-    barrier = pltpu.get_barrier_semaphore()
-    pl.semaphore_signal(barrier, inc=1, device_id=partner, device_id_type=MESH)
 
     @pl.when(odd == 1)
     def _():
@@ -136,6 +136,8 @@
             return carry
 
         lax.fori_loop(0, OWN, begin, 0)
+
+    reach_copy.start()
 
     @pl.when(odd == 0)
     def _():
@@ -209,14 +211,24 @@
     reach_copy.wait()
     lax.fori_loop(0, OWN, compute, 0)
 
+    def early_left():
+        first = done.at[pl.ds(0, EARLY), pl.ds(2, 2)]
+        remote(first.at[:, :, 0], first.at[:, :, 1], os_sem.at[1], or_sem, partner).wait_send()
+
     def gather(j, carry):
+        late = 1 + j // EARLY
+
+        @pl.when((j == EARLY) & (odd == 1))
+        def _():
+            early_left()
+
         remote(sent.at[j], got.at[j], gs_sem, gr_sem.at[j], partner).wait_recv()
         for part in range(2):
             total = local_grad[j, part]
             for way in range(2):
                 total = total + flat(got[j, way, part]).astype(jnp.float32)
             done[j, 2 + part] = tiled(total)
-            out_half(j, 2 + part).start()
+            out_half(j, 2 + part, late).start()
             out_own(j, 2 + part).start()
         return carry
 
@@ -226,7 +238,16 @@
     remote(near, got, ks_sem, kr_sem.at[0], partner).wait_send()
     remote(sent, got, gs_sem, gr_sem.at[0], partner).wait_send()
     pltpu.make_async_copy(done.at[:, :, 0], done.at[:, :, 1], ol_sem).wait()
-    remote(done.at[:, :, 1], done.at[:, :, 0], os_sem, or_sem, partner).wait()
+
+    @pl.when(odd == 0)
+    def _():
+        early_left()
+
+    both = done.at[:, pl.ds(0, 2)]
+    last = done.at[pl.ds(EARLY, OWN - EARLY), pl.ds(2, 2)]
+    remote(both.at[:, :, 0], both.at[:, :, 1], os_sem.at[0], or_sem, partner).wait_send()
+    remote(last.at[:, :, 0], last.at[:, :, 1], os_sem.at[2], or_sem, partner).wait_send()
+    remote(done.at[:, :, 1], done.at[:, :, 0], os_sem.at[0], or_sem, partner).wait_recv()
 
 
 def deliver(*refs):
@@ -265,7 +286,7 @@
             sems,
             sems((2,)), sems, sems((OWN, 2)),
             sems, sems((OWN,)), sems, sems((OWN,)),
-            sems, sems, sems,
+            sems((3,)), sems, sems,
             pltpu.SemaphoreType.REGULAR((2,)),
         ],
         compiler_params=pltpu.CompilerParams(

time: 43.7 us -> 43.7 us (level)
  no operation moved by 1% of the time
where the time goes in v6:
time: 43.7 us; the launch traced here: 43.5 us
  Pallas kernels  42.9 us (98%)
  between operations  0.64 us (1%)
    pallas_call x1, Pallas kernels, local(): pl.pallas_call(kernel, out_shape=[jax.ShapeDtypeStruct(shape, jnp.bfloat1...  41.6 us
    pallas_call x1, Pallas kernels, local(): pl.pallas_call(deliver, out_shape=[jax.ShapeDtypeStruct(shape, jnp.bfloat...  1.24 us

profile of v6, /device:TPU:24, one launch (start us, length us, event | category | flops | bytes accessed | tf_op | source)
XLA Modules:
  0.0 43.5 jit_solution(325649243488679621)
XLA Ops:
  0.6 41.6 %shard_map.84 = (bf16[6,6,12,4,128]{4,3,2,1,0:T(4,128)(2,1)S(1)}, bf16[6,6,12,4,128]{4,3,2,1,0:T(4,128)(2,1)S(1)}, bf16[6,6,12,4,128]{4,3,2,1,0:T(4,128)(2,1)S(1)}, bf16[6,6,12,4,128]{4,3,2,1,0:T(4,128)(2,1)S(1)}) custom-call(s32[2,12]{1,0:T(2,128)} %reach_in.1, bf16[6,6,12,4,128]{4,3,2,1,0:T(4,128)(2,1)} %bitcast.24, bf16[6,6,12,4,128]{4,3,2,1,0:T(4,128)(2,1)} %bitcast.25, ...), custom_call_target="tpu_custom_call" | custom-call | tf_op jit(solution)/shard_map/pallas_call | solution.py:273
  42.3 1.2 %shard_map.85 = (bf16[6,6,12,4,128]{4,3,2,1,0:T(4,128)(2,1)}, bf16[6,6,12,4,128]{4,3,2,1,0:T(4,128)(2,1)}, bf16[6,6,12,4,128]{4,3,2,1,0:T(4,128)(2,1)}, bf16[6,6,12,4,128]{4,3,2,1,0:T(4,128)(2,1)}) custom-call(bf16[6,6,12,4,128]{4,3,2,1,0:T(4,128)(2,1)S(1)} %get-tuple-element.12.refs_0_, bf16[6,6,12,4,128]{4,3,2,1,0:T(4,128)(2,1)S(1)} %get-tuple-element.13.refs_1_, ...), custom_call_target="tpu_custom_call" | custom-call | tf_op jit(solution)/shard_map/pallas_call | solution.py:296
